TPU v7x, 128 devices: a whole 4x4x4 slice. The times are simulated.
128 devices in a mesh: dp: 8 (over x, y_lo), tensor: 16 (over z, y_hi, core).
Axes of the slice: x: 4, y: 4 (y_hi: 2, y_lo: 2; y = y_hi * 2 + y_lo), z: 4, core: 2. Of those that a mesh axis runs over, the one named last changes fastest.
Arguments:
- grad_parts: bfloat16 [8, 14336, 4096], P('dp', 'tensor'), may hold values from -6 to 6
- master: float32 [14336, 4096], P('tensor', 'dp'), may hold values from -0.046875 to 0.046875
- moment_one: float32 [14336, 4096], P('tensor', 'dp'), may hold values from -3 to 3
- moment_two: float32 [14336, 4096], P('tensor', 'dp'), may hold values from 0.01 to 1
- gate_act: bfloat16 [8192, 14336], P('dp', 'tensor'), may hold values from -6 to 6
- up_act: bfloat16 [8192, 14336], P('dp', 'tensor'), may hold values from -6 to 6
Outputs:
- new_master: float32 [14336, 4096], P('tensor', 'dp')
- mixed: bfloat16 [8192, 4096], P('dp')
All inputs are finite; a program needn't handle non-finite values.
Results may differ from a plain program's by a relative error of at most 0.025.
Values may be sent and summed in bfloat16 or wider, within the bound.
A program may use at most 128 MiB of HBM per device.

v0:
```python
import math

import jax
import jax.numpy as jnp
from jax import lax
from jax.sharding import PartitionSpec as P

FF = 14336


beta_one = 0.9
beta_two = 0.95
epsilon = 1e-08
weight_decay = 0.1
step_count = 20


def per_device(grad_parts, master, moment_one, moment_two, gate_act, up_act):
    learn_rate = 0.8 / math.sqrt(FF)
    grad_sum = lax.psum_scatter(
        grad_parts[0].astype(jnp.float32).astype(jnp.bfloat16),
        "dp",
        scatter_dimension=1,
        tiled=True,
    ).astype(jnp.float32)
    moment_new = beta_one * moment_one + (1.0 - beta_one) * grad_sum
    square_new = beta_two * moment_two + (1.0 - beta_two) * grad_sum * grad_sum
    corr_one = 1.0 - beta_one**step_count
    corr_two = 1.0 - beta_two**step_count
    update = moment_new / corr_one / (jnp.sqrt(square_new / corr_two) + epsilon)
    new_master = master - learn_rate * (update + weight_decay * master)
    new_weights = new_master.astype(jnp.bfloat16)
    hidden = (jax.nn.silu(gate_act.astype(jnp.float32)) * up_act.astype(jnp.float32)).astype(
        jnp.bfloat16
    )
    whole_weights = lax.all_gather(new_weights, "dp", axis=1, tiled=True)
    mixed = lax.psum(
        jnp.dot(hidden, whole_weights, preferred_element_type=jnp.float32).astype(jnp.bfloat16),
        "tensor",
    )
    return (new_master, mixed)


def solution(mesh):
    in_specs = (
        P("dp", "tensor", None),
        P("tensor", "dp"),
        P("tensor", "dp"),
        P("tensor", "dp"),
        P("dp", "tensor"),
        P("dp", "tensor"),
    )
    out_specs = (P("tensor", "dp"), P("dp", None))
    return jax.shard_map(
        per_device, mesh=mesh, in_specs=in_specs, out_specs=out_specs, check_vma=False
    )
```

profile of v0, /device:TPU:1, one launch (start us, length us, event | category | flops | bytes accessed | tf_op | source)
XLA Modules:
  0.0 545.0 jit_solution(8395944076336469982)
XLA Ops:
  7.2 0.0 reduce-scatter.2.cloned.1.call-start
  7.2 0.0 copy-start
  7.2 0.7 reduce-scatter.2.cloned.1.call-update
  7.9 0.0 all-gather.2.cloned.1.call-start
  7.9 155.2 %reduce-scatter.2.cloned.1.call-done = bf16[896,512]{1,0:T(8,128)(2,1)} async-done(((bf16[896,4096]{1,0:T(8,128)(2,1)}), bf16[896,512]{1,0:T(8,128)(2,1)}) %reduce-scatter.2.cloned.1.call-update) | async-done | bytes 917520 | tf_op jit(solution)/shard_map/reduce_scatter | solution.py:20
  163.1 0.0 copy-done
  163.1 5.3 fusion.18
  168.5 0.0 all-gather.2.cloned.1.call-update
  168.5 0.0 all-reduce.2.cloned.1.call-start
  168.5 149.7 %all-gather.2.cloned.1.call-done = bf16[896,4096]{1,0:T(8,128)(2,1)} async-done(((bf16[896,512]{1,0:T(8,128)(2,1)}), bf16[896,4096]{1,0:T(8,128)(2,1)}) %all-gather.2.cloned.1.call-update) | async-done | bytes 7340048 | tf_op jit(solution)/shard_map/all_gather | solution.py:36
  318.2 14.7 %convolution_convert_fusion = bf16[1024,4096]{1,0:T(8,128)(2,1)} fusion(bf16[896,4096]{1,0:T(8,128)(2,1)} %all-gather.2.cloned.1.call-done, bf16[1024,896]{1,0:T(8,128)(2,1)} %param.11, bf16[1024,896]{1,0:T(8,128)(2,1)} %param.10), kind=kOutput, calls=%fused_computation | convolution fusion | flops 7527727104 | bytes 19398656 | tf_op jit(solution)/shard_map/dot_general | solution.py:38
  332.9 0.0 all-reduce.2.cloned.1.call-update
  332.9 197.6 %all-reduce.2.cloned.1.call-done = bf16[1024,4096]{1,0:T(8,128)(2,1)} async-done(((bf16[1024,4096]{1,0:T(8,128)(2,1)}), bf16[1024,4096]{1,0:T(8,128)(2,1)}) %all-reduce.2.cloned.1.call-update) | async-done | bytes 8388624 | tf_op jit(solution)/shard_map/psum | solution.py:37
  530.6 7.9 %copy.9 = bf16[1024,4096]{1,0:T(8,128)(2,1)} copy(bf16[1024,4096]{1,0:T(8,128)(2,1)} %all-reduce.2.cloned.1.call-done) | data formatting | bytes 16777216
Async XLA Ops:
  7.2 156.0 %reduce-scatter.2.cloned.1.call-start = ((), (), s32[]{:S(2)}) async-start(), calls=%async_computation.1 | async-start | bytes 8257536 | tf_op jit(solution)/shard_map/reduce_scatter | solution.py:20
  7.2 155.9 %copy-start = (f32[896,512]{1,0:T(8,128)S(1)}, f32[896,512]{1,0:T(8,128)}, u32[]{:S(2)}) copy-start(f32[896,512]{1,0:T(8,128)} %param.7) | copy-start | bytes 5505028
  7.9 310.3 %all-gather.2.cloned.1.call-start = ((), (), s32[]{:S(2)}) async-start(), calls=%async_computation.2 | async-start | bytes 8257536 | tf_op jit(solution)/shard_map/all_gather | solution.py:36
  168.5 362.1 %all-reduce.2.cloned.1.call-start = ((), (), s32[]{:S(2)}) async-start(), calls=%async_computation.3 | async-start | bytes 16777216 | tf_op jit(solution)/shard_map/psum | solution.py:37
Sparse Core Ops, SparseCore 0:
  10.4 152.6 reduce-scatter.1
  168.6 149.5 all-gather.1
  333.1 197.4 all-reduce.1
where the time goes:
time: 546 us; the launch traced here: 545 us
  waiting for transfers between devices  503 us (92%)
  matrix products  14.7 us (3%)
  between operations  13.8 us (3%)
  local copies, waits for them, and re-layouts  7.89 us (1%)
    psum x1, waiting for transfers between devices, per_device(): lax.psum(jnp.dot(hidden, whole_weights, preferred_element_type=jnp.float3...  198 us
    reduce_scatter x1, waiting for transfers between devices, per_device(): lax.psum_scatter(grad_parts[0].astype(jnp.float32).astype(jnp.bfloat16),...  155 us
    all_gather x1, waiting for transfers between devices, per_device(): whole_weights = lax.all_gather(new_weights, 'dp', axis=1, tiled=True)  150 us
    dot_general x1, matrix products, per_device(): jnp.dot(hidden, whole_weights, preferred_element_type=jnp.float32)  14.7 us
  transfers between devices with their start and end apart: 3, of which 3 were waited for; matrix products, arithmetic and copies ran while one was open for 0% of the time, Pallas kernels for 0%

commit v1 on v0

v1 whole, which is shorter than its diff:
```python
import functools
import math

import jax
import jax.numpy as jnp
from jax import lax
from jax.experimental import pallas as pl
from jax.experimental.pallas import tpu as pltpu
from jax.sharding import PartitionSpec as P

FF = 14336

beta_one = 0.9
beta_two = 0.95
epsilon = 1e-08
weight_decay = 0.1
step_count = 20

MESH = pl.DeviceIdType.MESH
F32 = jnp.float32
BF16 = jnp.bfloat16

K = 4
LANES = 128
HP = 8


def sweep(rows, tile, body):
    if rows == tile:
        body(0)
        return

    @pl.loop(0, rows // tile)
    def _(i):
        body(pl.multiple_of(i * tile, tile))


def kernel(
    g, mst, mom, sqr, gate, up,
    nm_out, mix_out,
    gown, gfw, r1, r2, sy, ry, mst_v, mom_v, sqr_v, w, gate_v, up_v, hid,
    p, rc, zr1, zr2, yb, yr, out,
    ld, nms, outs_sem,
    x1s, x1r, rws, rwr, x2s, x2r, ys, yrs, a1s, a1r, a2s, a2r, hs, hr,
    cs, cr, z1s, z1r, zws, zwr, z2s, z2r, y3s, y3r, o1s, o1r, o2s, o2r, ocs, ocr,
):
    dp, t = lax.axis_index("dp"), lax.axis_index("tensor")
    x, yl = lax.div(dp, 2), lax.rem(dp, 2)
    z, yh, c = lax.div(t, 4), lax.rem(lax.div(t, 2), 2), lax.rem(t, 2)
    xn, xp = lax.rem(x + 1, 4), lax.rem(x + 3, 4)
    xo = lax.rem(x + 2, 4)
    zn, zp = lax.rem(z + 1, 4), lax.rem(z + 3, 4)
    zo = lax.rem(z + 2, 4)

    def dev(x=x, yl=yl, z=z, yh=yh, c=c):
        return (x * 2 + yl, z * 4 + yh * 2 + c)

    X = (dev(x=xn), dev(x=xp))
    Z = (dev(z=zn), dev(z=zp))
    YL = dev(yl=1 - yl)
    YH = dev(yh=1 - yh)
    YD = dev(yl=1 - yl, yh=1 - yh)
    C = dev(c=1 - c)

    rows = gown.shape[1]
    half = rows // 2
    tokens = hid.shape[1]
    wide = p.shape[3]
    core_rows = tokens // 2
    zrows = core_rows // 4
    zh = zrows // 2

    sends = []
    done = {}

    def remote(src, dst, s, r, to):
        cp = pltpu.make_async_remote_copy(
            src_ref=src, dst_ref=dst, send_sem=s, recv_sem=r, device_id=to, device_id_type=MESH
        )
        cp.start()
        sends.append(cp)
        return cp

    def columns(owner, strip, k, width=LANES):
        return pl.ds(pl.multiple_of(owner * (2 * K * LANES) + strip * (K * LANES) + k * LANES, LANES), width)

    loads = {}

    def load(name, i, src, dst):
        cp = pltpu.make_async_copy(src, dst, ld.at[i])
        cp.start()
        loads[name] = cp

    block = K * LANES
    load("f0", 0, g.at[0, :, columns(xn, 0, 0, block)], gfw.at[0])
    load("f1", 1, g.at[0, :, columns(xp, 1, 0, block)], gfw.at[1])
    load("gate", 2, gate, gate_v)
    load("up", 3, up, up_v)
    load("own0", 4, g.at[0, :, columns(x, 0, 0, block)], gown.at[0])
    load("own1", 5, g.at[0, :, columns(x, 1, 0, block)], gown.at[1])
    load("mst", 6, mst, mst_v)
    load("mom", 7, mom, mom_v)
    load("sqr", 8, sqr, sqr_v)

    def loaded(*names):
        for n in names:
            if n in loads:
                loads.pop(n).wait()

    barrier = pltpu.get_barrier_semaphore()
    friends = (*X, *Z, YL, YH, YD, C)
    for d in friends:
        pl.semaphore_signal(barrier, inc=1, device_id=d, device_id_type=MESH)
    pl.semaphore_wait(barrier, len(friends))

    def X1(k):
        done["x1", 0, k] = remote(
            g.at[0, :, columns(xo, 0, k)], r1.at[0, k], x1s.at[0, k], x1r.at[0, k], X[0])
        done["x1", 1, k] = remote(
            g.at[0, :, columns(xo, 1, k)], r1.at[1, k], x1s.at[1, k], x1r.at[1, k], X[1])

    def R(k):
        done["rw", 0, k] = remote(
            g.at[0, :, columns(xn, 1, k)], r2.at[0, k, 1], rws.at[0, k], rwr.at[0, k], X[0])
        done["rw", 1, k] = remote(
            g.at[0, :, columns(xp, 0, k)], r2.at[1, k, 0], rws.at[1, k], rwr.at[1, k], X[1])

    def X2(k):
        loaded("f0", "f1")
        cols = pl.ds(k * LANES, LANES)
        for d in (0, 1):
            done["x1", d, k].wait_recv()

            def body(r):
                at = pl.ds(r, 128)
                gfw[d, at, cols] = (gfw[d, at, cols].astype(F32) + r1[d, k, at, :].astype(F32)).astype(BF16)

            sweep(rows, 128, body)
            done["x2", d, k] = remote(
                gfw.at[d, :, cols], r2.at[d, k, d], x2s.at[d, k], x2r.at[d, k], X[d])

    def X3(k):
        loaded("own0", "own1")
        for d in (0, 1):
            done["rw", d, k].wait_recv()
            done["x2", d, k].wait_recv()
        cols = pl.ds(k * LANES, LANES)
        other = 1 - yl

        def body(r):
            at = pl.ds(r, 128)
            sy[k, at, :] = (
                gown[other, at, cols].astype(F32)
                + r2[0, k, other, at, :].astype(F32)
                + r2[1, k, other, at, :].astype(F32)
            ).astype(BF16)

        sweep(rows, 128, body)
        done["y", k] = remote(sy.at[k], ry.at[k], ys.at[k], yrs.at[k], YL)

    learn_rate = 0.8 / math.sqrt(FF)
    corr_one = 1.0 - beta_one**step_count
    corr_two = 1.0 - beta_two**step_count

    def Y1(k):
        loaded("mst", "mom", "sqr")
        done["y", k].wait_recv()
        cols = pl.ds(k * LANES, LANES)

        def body(r):
            at = pl.ds(r, 64)
            grad = (
                gown[yl, at, cols].astype(F32)
                + r2[0, k, yl, at, :].astype(F32)
                + r2[1, k, yl, at, :].astype(F32)
                + ry[k, at, :].astype(F32)
            )
            moment_new = beta_one * mom_v[at, cols] + (1.0 - beta_one) * grad
            square_new = beta_two * sqr_v[at, cols] + (1.0 - beta_two) * grad * grad
            update = moment_new / corr_one / (jnp.sqrt(square_new / corr_two) + epsilon)
            old = mst_v[at, cols]
            new = old - learn_rate * (update + weight_decay * old)
            mst_v[at, cols] = new
            w[k, x, at, :] = new.astype(BF16)

        sweep(rows, 64, body)
        for d in (0, 1):
            done["a1", d, k] = remote(
                w.at[k, x], w.at[k, x], a1s.at[d, k], a1r.at[d, k], X[d])
        cp = pltpu.make_async_copy(mst_v.at[:, cols], nm_out.at[:, cols], nms.at[k])
        cp.start()
        done["nm", k] = cp

    def A2(k):
        for d, origin in ((0, xp), (1, xn)):
            done["a1", d, k].wait_recv()
            at = pl.ds(d * half, half)
            done["a2", d, k] = remote(
                w.at[k, origin, at], w.at[k, origin, at], a2s.at[d, k], a2r.at[d, k], X[d])

    piece = tokens // HP

    def HID():
        loaded("gate", "up")

        def body(r):
            at = pl.ds(r, 32)
            v = gate_v[at, :].astype(F32)
            hid[0, at, :] = (v / (1.0 + jnp.exp(-v)) * up_v[at, :].astype(F32)).astype(BF16)

        sweep(tokens, 32, body)

    def H(i):
        at = pl.ds(i * piece, piece)
        done["h", i] = remote(hid.at[0, at], hid.at[1, at], hs.at[i], hr.at[i], YL)

    def M(k, h):
        if h == 0:
            for d in (0, 1):
                done["a2", d, k].wait_recv()
        elif k == 0:
            for i in range(HP):
                done["h", i].wait_recv()
        for part in (1 - c, c):
            def body(r):
                at = pl.ds(pl.multiple_of(part * core_rows + r, 256), 256)
                weights = jnp.concatenate([w[k, j] for j in range(4)], axis=1)
                p[k, h, at, :] = jnp.dot(
                    hid[h, at, :], weights, preferred_element_type=F32).astype(BF16)

            sweep(core_rows, 256, body)
            if part is not c:
                at = pl.ds(pl.multiple_of((1 - c) * core_rows, core_rows), core_rows)
                done["c", k, h] = remote(p.at[k, h, at], rc.at[k, h], cs.at[k, h], cr.at[k, h], C)

    base = c * core_rows

    def zat(owner, part, count):
        return pl.ds(pl.multiple_of(base + owner * zrows + part * zh, zh), count)

    def Z0(k, h):
        done["c", k, h].wait_recv()

        def body(r):
            at = pl.ds(pl.multiple_of(base + r, 64), 64)
            p[k, h, at, :] = (p[k, h, at, :].astype(F32) + rc[k, h, pl.ds(r, 64), :].astype(F32)).astype(BF16)

        sweep(core_rows, 64, body)
        for d in (0, 1):
            done["z1", d, k, h] = remote(
                p.at[k, h, zat(zo, d, zh)], zr1.at[d, k, h], z1s.at[d, k, h], z1r.at[d, k, h], Z[d])
        for d, owner in ((0, zn), (1, zp)):
            done["zw", d, k, h] = remote(
                p.at[k, h, zat(owner, 1 - d, zh)], zr2.at[d, k, h, pl.ds((1 - d) * zh, zh)],
                zws.at[d, k, h], zwr.at[d, k, h], Z[d])

    def Z2(k, h):
        for d, owner in ((0, zn), (1, zp)):
            done["z1", d, k, h].wait_recv()
            at = zat(owner, d, zh)
            p[k, h, at, :] = (p[k, h, at, :].astype(F32) + zr1[d, k, h].astype(F32)).astype(BF16)
            done["z2", d, k, h] = remote(
                p.at[k, h, at], zr2.at[d, k, h, pl.ds(d * zh, zh)], z2s.at[d, k, h], z2r.at[d, k, h], Z[d])

    def Z3(k, h):
        for d in (0, 1):
            done["zw", d, k, h].wait_recv()
            done["z2", d, k, h].wait_recv()
        for part in (0, 1):
            at = pl.ds(part * zh, zh)
            yb[k, h, at, :] = (
                p[k, h, zat(z, part, zh), :].astype(F32)
                + zr2[0, k, h, at, :].astype(F32)
                + zr2[1, k, h, at, :].astype(F32)
            ).astype(BF16)
        for i, to in ((0, YH),) if h == 0 else ((1, YL), (2, YD)):
            done["y3", k, i] = remote(yb.at[k, h], yr.at[k, i], y3s.at[k, i], y3r.at[k, i], to)

    def oat(owner, part, count):
        return pl.ds(pl.multiple_of(base + owner * zrows + part * zh, zh), count)

    def Y2(k, h):
        group = yl if h == 0 else 1 - yl
        for i in (0,) if h == 0 else (1, 2):
            done["y3", k, i].wait_recv()
        for part in (0, 1):
            at = pl.ds(part * zh, zh)
            if h == 0:
                total = yb[k, 0, at, :].astype(F32) + yr[k, 0, at, :].astype(F32)
            else:
                total = yr[k, 1, at, :].astype(F32) + yr[k, 2, at, :].astype(F32)
            out[k, group, oat(z, part, zh), :] = total.astype(BF16)
        mine = out.at[k, group, oat(z, 0, zrows)]
        for d in (0, 1):
            done["o1", d, k, h] = remote(mine, mine, o1s.at[d, k, h], o1r.at[d, k, h], Z[d])

    def O2(k, h):
        group = yl if h == 0 else 1 - yl
        for d, origin in ((0, zp), (1, zn)):
            done["o1", d, k, h].wait_recv()
            part = out.at[k, group, oat(origin, d, zh)]
            done["o2", d, k, h] = remote(part, part, o2s.at[d, k, h], o2r.at[d, k, h], Z[d])

    def O3(k, h):
        group = yl if h == 0 else 1 - yl
        for d in (0, 1):
            done["o2", d, k, h].wait_recv()
        part = out.at[k, group, pl.ds(pl.multiple_of(base, core_rows), core_rows)]
        done["oc", k, h] = remote(part, part, ocs.at[k, h], ocr.at[k, h], C)

    def E(k, h):
        group = yl if h == 0 else 1 - yl
        done["oc", k, h].wait_recv()
        for j in range(4):
            cp = pltpu.make_async_copy(
                out.at[k, group, :, pl.ds(j * LANES, LANES)],
                mix_out.at[:, columns(j, group, k)], outs_sem.at[k, h, j])
            cp.start()
            done["e", k, h, j] = cp

    X1(0), R(0)
    HID()
    H(0), H(1), H(2)
    X2(0), X1(1), R(1)
    X3(0), H(3), H(4)
    X2(1), X1(2)
    Y1(0)
    R(2), H(5)
    X3(1)
    A2(0)
    H(6), H(7)
    X2(2), X1(3)
    M(0, 0)
    Y1(1)
    R(3)
    Z0(0, 0)
    A2(1)
    Z2(0, 0)
    X3(2)
    M(0, 1)
    Z3(0, 0)
    Z0(0, 1)
    X2(3)
    Y2(0, 0)
    M(1, 0)
    Z2(0, 1)
    Z0(1, 0)
    Y1(2)
    O2(0, 0)
    Z3(0, 1)
    M(1, 1)
    Z2(1, 0)
    Z0(1, 1)
    Y2(0, 1)
    O3(0, 0)
    X3(3)
    A2(2)
    Z3(1, 0)
    Z2(1, 1)
    O2(0, 1)
    E(0, 0)
    Y2(1, 0)
    Z3(1, 1)
    O3(0, 1)
    Y1(3)
    M(2, 0)
    Z0(2, 0)
    O2(1, 0)
    Y2(1, 1)
    M(2, 1)
    Z0(2, 1)
    A2(3)
    E(0, 1)
    Z2(2, 0)
    O3(1, 0)
    O2(1, 1)
    Z2(2, 1)
    Z3(2, 0)
    M(3, 0)
    Z0(3, 0)
    Z3(2, 1)
    M(3, 1)
    Z0(3, 1)
    Y2(2, 0)
    E(1, 0)
    O3(1, 1)
    Z2(3, 0)
    Y2(2, 1)
    O2(2, 0)
    Z2(3, 1)
    Z3(3, 0)
    E(1, 1)
    O2(2, 1)
    O3(2, 0)
    Z3(3, 1)
    Y2(3, 0)
    O3(2, 1)
    E(2, 0)
    Y2(3, 1)
    O2(3, 0)
    E(2, 1)
    O2(3, 1)
    O3(3, 0)
    O3(3, 1)
    E(3, 0)
    E(3, 1)

    for cp in sends:
        cp.wait_send()
    for key, cp in done.items():
        if key[0] in ("nm", "e"):
            cp.wait()


def per_device(grad_parts, master, moment_one, moment_two, gate_act, up_act):
    _, rows, width = grad_parts.shape
    tokens = gate_act.shape[0]
    hbm = pl.BlockSpec(memory_space=pl.ANY)
    block = K * LANES
    vm = pltpu.VMEM
    dma = pltpu.SemaphoreType.DMA

    def pair(shape):
        return [dma(shape), dma(shape)]

    return pl.pallas_call(
        kernel,
        out_shape=(
            jax.ShapeDtypeStruct(master.shape, F32),
            jax.ShapeDtypeStruct((tokens, width), BF16),
        ),
        in_specs=[hbm] * 6,
        out_specs=(hbm, hbm),
        scratch_shapes=[
            vm((2, rows, block), BF16),
            vm((2, rows, block), BF16),
            vm((2, K, rows, LANES), BF16),
            vm((2, K, 2, rows, LANES), BF16),
            vm((K, rows, LANES), BF16),
            vm((K, rows, LANES), BF16),
            vm((rows, block), F32),
            vm((rows, block), F32),
            vm((rows, block), F32),
            vm((K, 4, rows, LANES), BF16),
            vm((tokens, rows), BF16),
            vm((tokens, rows), BF16),
            vm((2, tokens, rows), BF16),
            vm((K, 2, tokens, block), BF16),
            vm((K, 2, tokens // 2, block), BF16),
            vm((2, K, 2, tokens // 16, block), BF16),
            vm((2, K, 2, tokens // 8, block), BF16),
            vm((K, 2, tokens // 8, block), BF16),
            vm((K, 3, tokens // 8, block), BF16),
            vm((K, 2, tokens, block), BF16),
            dma((9,)), dma((K,)), dma((K, 2, 4)),
            *pair((2, K)), *pair((2, K)), *pair((2, K)), *pair((K,)),
            *pair((2, K)), *pair((2, K)), *pair((HP,)),
            *pair((K, 2)), *pair((2, K, 2)), *pair((2, K, 2)), *pair((2, K, 2)),
            *pair((K, 3)), *pair((2, K, 2)), *pair((2, K, 2)), *pair((K, 2)),
        ],
        compiler_params=pltpu.CompilerParams(
            collective_id=0, has_side_effects=True, vmem_limit_bytes=62 * 2**20
        ),
        name="handover",
    )(grad_parts, master, moment_one, moment_two, gate_act, up_act)


def solution(mesh):
    in_specs = (
        P("dp", "tensor", None),
        P("tensor", "dp"),
        P("tensor", "dp"),
        P("tensor", "dp"),
        P("dp", "tensor"),
        P("dp", "tensor"),
    )
    out_specs = (P("tensor", "dp"), P("dp", None))
    return jax.shard_map(
        per_device, mesh=mesh, in_specs=in_specs, out_specs=out_specs, check_vma=False
    )
```

time: 546 us -> 172 us (0.32)
  waiting for transfers between devices: 503 us -> 0 us
  Pallas kernels: 0 us -> 161 us
  matrix products: 14.7 us -> 0 us
  between operations: 13.8 us -> 0.64 us
    psum x1 -> x0, waiting for transfers between devices: 198 us -> none  [per_device(): lax.psum(jnp.dot(hidden, whole_weights, preferred_element_type=jnp.float3...]
    pallas_call x0 -> x1, Pallas kernels: none -> 161 us  [per_device(): pl.pallas_call(kernel, out_shape=(jax.ShapeDtypeStruct(master.shape, F32)...]
    reduce_scatter x1 -> x0, waiting for transfers between devices: 155 us -> none  [per_device(): lax.psum_scatter(grad_parts[0].astype(jnp.float32).astype(jnp.bfloat16),...]
    all_gather x1 -> x0, waiting for transfers between devices: 150 us -> none  [per_device(): whole_weights = lax.all_gather(new_weights, 'dp', axis=1, tiled=True)]
    dot_general x1 -> x0, matrix products: 14.7 us -> none  [per_device(): jnp.dot(hidden, whole_weights, preferred_element_type=jnp.float32)]
  transfers between devices with their start and end apart: 3 -> 0, of which waited for: 3 -> 0; matrix products, arithmetic and copies ran while one was open for 0% -> 0% of each run, Pallas kernels for 0% -> 0%
where the time goes in v1:
time: 172 us
  Pallas kernels  161 us (94%)
  local copies, waits for them, and re-layouts  10.8 us (6%)
    pallas_call x1, Pallas kernels, per_device(): pl.pallas_call(kernel, out_shape=(jax.ShapeDtypeStruct(master.shape, F32)...  161 us
    unnamed x2, local copies, waits for them, and re-layouts  10.8 us

profile of v1, /device:TPU:1, one launch (start us, length us, event | category | flops | bytes accessed | tf_op | source)
XLA Modules:
  0.0 172.3 jit_solution(15909685667860760767)
XLA Ops:
  0.6 160.9 %handover.1 = (f32[896,512]{1,0:T(8,128)}, bf16[1024,4096]{1,0:T(8,128)(2,1)}) custom-call(bf16[1,896,4096]{2,1,0:T(8,128)(2,1)} %g.1, f32[896,512]{1,0:T(8,128)} %mst.1, f32[896,512]{1,0:T(8,128)} %mom.1, f32[896,512]{1,0:T(8,128)} %sqr.1, bf16[1024,896]{1,0:T(8,128)(2,1)} %gate.1, bf16[1024,896]{1,0:T(8,128)(2,1)} %up.1), custom_call_target="tpu_custom_call" | custom-call | tf_op jit(solution)/shard_map/handover/pallas_call | solution.py:426
  161.5 2.9 %copy.10 = f32[896,512]{1,0:T(8,128)} copy(f32[896,512]{1,0:T(8,128)} %get-tuple-element.4) | data formatting | bytes 3670016
  164.4 7.9 %copy.11 = bf16[1024,4096]{1,0:T(8,128)(2,1)} copy(bf16[1024,4096]{1,0:T(8,128)(2,1)} %get-tuple-element.5) | data formatting | bytes 16777216

commit v2 on v1

--- a/solution.py
+++ b/solution.py
@@ -35,12 +35,30 @@
         body(pl.multiple_of(i * tile, tile))
 
 
+def plan():
+    return [
+        ("X1", 2), ("R", 3), ("HID",), ("X1", 3), ("H", 0), ("H", 4), ("H", 2), ("R", 2), ("X2", 2), ("X2", 3),
+        ("H", 6), ("X1", 1), ("X3", 2), ("X3", 3), ("H", 1), ("H", 3), ("H", 5), ("Y1", 2), ("Y1", 3),
+        ("A2", 2), ("A2", 3), ("R", 1), ("X2", 1), ("X1", 0), ("H", 7), ("M", 2, 0), ("M", 3, 0), ("Z0", 2, 0),
+        ("Z0", 3, 0), ("M", 2, 1), ("R", 0), ("Z2", 2, 0), ("X3", 1), ("Z2", 3, 0), ("Z0", 2, 1), ("M", 3, 1),
+        ("Z3", 2, 0), ("Z2", 2, 1), ("Z3", 3, 0), ("X2", 0), ("Z0", 3, 1), ("Z3", 2, 1), ("Y2", 2, 0),
+        ("Y1", 1), ("Y2", 3, 0), ("X3", 0), ("Z2", 3, 1), ("Y2", 2, 1), ("O2", 2, 0), ("O2", 3, 0), ("A2", 1),
+        ("Z3", 3, 1), ("Y1", 0), ("O2", 2, 1), ("M", 1, 0), ("Y2", 3, 1), ("M", 1, 1), ("Z0", 1, 0), ("A2", 0),
+        ("Z0", 1, 1), ("O2", 3, 1), ("M", 0, 0), ("Z2", 1, 0), ("Z2", 1, 1), ("M", 0, 1), ("Z0", 0, 0),
+        ("Z3", 1, 0), ("O3", 3, 1), ("Z0", 0, 1), ("Z3", 1, 1), ("E", 3, 1), ("Z2", 0, 0), ("Z2", 0, 1),
+        ("O3", 2, 0), ("O3", 2, 1), ("Y2", 1, 0), ("Z3", 0, 0), ("Y2", 1, 1), ("Z3", 0, 1), ("O2", 1, 0),
+        ("Y2", 0, 0), ("O3", 3, 0), ("E", 2, 0), ("Y2", 0, 1), ("O2", 1, 1), ("O3", 1, 0), ("E", 2, 1),
+        ("O2", 0, 0), ("E", 3, 0), ("O2", 0, 1), ("O3", 1, 1), ("O3", 0, 0), ("O3", 0, 1), ("E", 0, 0),
+        ("E", 1, 0), ("E", 1, 1), ("E", 0, 1),
+    ]
+
+
 def kernel(
     g, mst, mom, sqr, gate, up,
-    nm_out, mix_out,
-    gown, gfw, r1, r2, sy, ry, mst_v, mom_v, sqr_v, w, gate_v, up_v, hid,
-    p, rc, zr1, zr2, yb, yr, out,
-    ld, nms, outs_sem,
+    mst_v, out,
+    gown, gfw, r1, r2, sy, ry, mom_v, sqr_v, w, gate_v, up_v, hid,
+    p, rc, zr1, zr2, yb, yr,
+    ld,
     x1s, x1r, rws, rwr, x2s, x2r, ys, yrs, a1s, a1r, a2s, a2r, hs, hr,
     cs, cr, z1s, z1r, zws, zwr, z2s, z2r, y3s, y3r, o1s, o1r, o2s, o2r, ocs, ocr,
 ):
@@ -187,9 +205,6 @@
         for d in (0, 1):
             done["a1", d, k] = remote(
                 w.at[k, x], w.at[k, x], a1s.at[d, k], a1r.at[d, k], X[d])
-        cp = pltpu.make_async_copy(mst_v.at[:, cols], nm_out.at[:, cols], nms.at[k])
-        cp.start()
-        done["nm", k] = cp
 
     def A2(k):
         for d, origin in ((0, xp), (1, xn)):
@@ -218,9 +233,9 @@
         if h == 0:
             for d in (0, 1):
                 done["a2", d, k].wait_recv()
-        elif k == 0:
+        elif ("h", 0) in done:
             for i in range(HP):
-                done["h", i].wait_recv()
+                done.pop(("h", i)).wait_recv()
         for part in (1 - c, c):
             def body(r):
                 at = pl.ds(pl.multiple_of(part * core_rows + r, 256), 256)
@@ -309,107 +324,28 @@
         done["oc", k, h] = remote(part, part, ocs.at[k, h], ocr.at[k, h], C)
 
     def E(k, h):
-        group = yl if h == 0 else 1 - yl
         done["oc", k, h].wait_recv()
-        for j in range(4):
-            cp = pltpu.make_async_copy(
-                out.at[k, group, :, pl.ds(j * LANES, LANES)],
-                mix_out.at[:, columns(j, group, k)], outs_sem.at[k, h, j])
-            cp.start()
-            done["e", k, h, j] = cp
-
-    X1(0), R(0)
-    HID()
-    H(0), H(1), H(2)
-    X2(0), X1(1), R(1)
-    X3(0), H(3), H(4)
-    X2(1), X1(2)
-    Y1(0)
-    R(2), H(5)
-    X3(1)
-    A2(0)
-    H(6), H(7)
-    X2(2), X1(3)
-    M(0, 0)
-    Y1(1)
-    R(3)
-    Z0(0, 0)
-    A2(1)
-    Z2(0, 0)
-    X3(2)
-    M(0, 1)
-    Z3(0, 0)
-    Z0(0, 1)
-    X2(3)
-    Y2(0, 0)
-    M(1, 0)
-    Z2(0, 1)
-    Z0(1, 0)
-    Y1(2)
-    O2(0, 0)
-    Z3(0, 1)
-    M(1, 1)
-    Z2(1, 0)
-    Z0(1, 1)
-    Y2(0, 1)
-    O3(0, 0)
-    X3(3)
-    A2(2)
-    Z3(1, 0)
-    Z2(1, 1)
-    O2(0, 1)
-    E(0, 0)
-    Y2(1, 0)
-    Z3(1, 1)
-    O3(0, 1)
-    Y1(3)
-    M(2, 0)
-    Z0(2, 0)
-    O2(1, 0)
-    Y2(1, 1)
-    M(2, 1)
-    Z0(2, 1)
-    A2(3)
-    E(0, 1)
-    Z2(2, 0)
-    O3(1, 0)
-    O2(1, 1)
-    Z2(2, 1)
-    Z3(2, 0)
-    M(3, 0)
-    Z0(3, 0)
-    Z3(2, 1)
-    M(3, 1)
-    Z0(3, 1)
-    Y2(2, 0)
-    E(1, 0)
-    O3(1, 1)
-    Z2(3, 0)
-    Y2(2, 1)
-    O2(2, 0)
-    Z2(3, 1)
-    Z3(3, 0)
-    E(1, 1)
-    O2(2, 1)
-    O3(2, 0)
-    Z3(3, 1)
-    Y2(3, 0)
-    O3(2, 1)
-    E(2, 0)
-    Y2(3, 1)
-    O2(3, 0)
-    E(2, 1)
-    O2(3, 1)
-    O3(3, 0)
-    O3(3, 1)
-    E(3, 0)
-    E(3, 1)
+
+    steps = dict(X1=X1, R=R, X2=X2, X3=X3, Y1=Y1, A2=A2, HID=HID, H=H, M=M, Z0=Z0, Z2=Z2, Z3=Z3, Y2=Y2, O2=O2, O3=O3, E=E)
+    for name, *at in plan():
+        steps[name](*at)
 
     for cp in sends:
         cp.wait_send()
-    for key, cp in done.items():
-        if key[0] in ("nm", "e"):
-            cp.wait()
+
+
+def place(nm, out, nm_out, mix_out, sems):
+    copies = [pltpu.make_async_copy(nm, nm_out, sems.at[0])]
+    for k in range(K):
+        for group in (0, 1):
+            for j in range(4):
+                at = pl.ds((j * 2 * K + group * K + k) * LANES, LANES)
+                copies.append(pltpu.make_async_copy(
+                    out.at[k, group, :, pl.ds(j * LANES, LANES)], mix_out.at[:, at], sems.at[len(copies)]))
+    for cp in copies:
+        cp.start()
+    for cp in copies:
+        cp.wait()
 
 
 def per_device(grad_parts, master, moment_one, moment_two, gate_act, up_act):
@@ -423,14 +359,13 @@
     def pair(shape):
         return [dma(shape), dma(shape)]
 
-    return pl.pallas_call(
+    new_master, mixed = pl.pallas_call(
         kernel,
         out_shape=(
-            jax.ShapeDtypeStruct(master.shape, F32),
-            jax.ShapeDtypeStruct((tokens, width), BF16),
+            vm(master.shape, F32),
+            vm((K, 2, tokens, block), BF16),
         ),
         in_specs=[hbm] * 6,
-        out_specs=(hbm, hbm),
         scratch_shapes=[
             vm((2, rows, block), BF16),
             vm((2, rows, block), BF16),
@@ -438,7 +373,6 @@
             vm((2, K, 2, rows, LANES), BF16),
             vm((K, rows, LANES), BF16),
             vm((K, rows, LANES), BF16),
-            vm((rows, block), F32),
             vm((rows, block), F32),
             vm((rows, block), F32),
             vm((K, 4, rows, LANES), BF16),
@@ -451,18 +385,29 @@
             vm((2, K, 2, tokens // 8, block), BF16),
             vm((K, 2, tokens // 8, block), BF16),
             vm((K, 3, tokens // 8, block), BF16),
-            vm((K, 2, tokens, block), BF16),
-            dma((9,)), dma((K,)), dma((K, 2, 4)),
+            dma((9,)),
             *pair((2, K)), *pair((2, K)), *pair((2, K)), *pair((K,)),
             *pair((2, K)), *pair((2, K)), *pair((HP,)),
             *pair((K, 2)), *pair((2, K, 2)), *pair((2, K, 2)), *pair((2, K, 2)),
             *pair((K, 3)), *pair((2, K, 2)), *pair((2, K, 2)), *pair((K, 2)),
         ],
         compiler_params=pltpu.CompilerParams(
-            collective_id=0, has_side_effects=True, vmem_limit_bytes=62 * 2**20
+            collective_id=0, has_side_effects=True, vmem_limit_bytes=50 * 2**20
         ),
         name="handover",
     )(grad_parts, master, moment_one, moment_two, gate_act, up_act)
+    return pl.pallas_call(
+        place,
+        out_shape=(
+            jax.ShapeDtypeStruct(master.shape, F32),
+            jax.ShapeDtypeStruct((tokens, width), BF16),
+        ),
+        in_specs=[hbm] * 2,
+        out_specs=(hbm, hbm),
+        scratch_shapes=[dma((1 + 8 * K,))],
+        compiler_params=pltpu.CompilerParams(vmem_limit_bytes=2**20),
+        name="place",
+    )(pltpu.with_memory_space_constraint(new_master, vm), pltpu.with_memory_space_constraint(mixed, vm))
 
 
 def solution(mesh):

time: 172 us -> 147 us (0.85)
  Pallas kernels: 161 us -> 147 us
  local copies, waits for them, and re-layouts: 10.8 us -> 0 us
    pallas_call x1 -> x2, Pallas kernels: 161 us -> 147 us  [the longest x1 143 us: per_device(): pl.pallas_call(kernel, out_shape=(vm(master.shape, F32), vm((K, 2, tokens...]
    unnamed x2 -> x0, local copies, waits for them, and re-layouts: 10.8 us -> none
where the time goes in v2:
time: 147 us
  Pallas kernels  147 us (100%)
    pallas_call x1, Pallas kernels, per_device(): pl.pallas_call(kernel, out_shape=(vm(master.shape, F32), vm((K, 2, tokens...  143 us
    pallas_call x1, Pallas kernels, per_device(): pl.pallas_call(place, out_shape=(jax.ShapeDtypeStruct(master.shape, F32),...  4.1 us

profile of v2, /device:TPU:1, one launch (start us, length us, event | category | flops | bytes accessed | tf_op | source)
XLA Modules:
  0.0 147.4 jit_solution(9929237694064827194)
XLA Ops:
  0.6 142.6 %handover.1 = (f32[896,512]{1,0:T(8,128)S(1)}, bf16[4,2,1024,512]{3,2,1,0:T(8,128)(2,1)S(1)}) custom-call(bf16[1,896,4096]{2,1,0:T(8,128)(2,1)} %g.1, f32[896,512]{1,0:T(8,128)} %mst.1, f32[896,512]{1,0:T(8,128)} %mom.1, f32[896,512]{1,0:T(8,128)} %sqr.1, bf16[1024,896]{1,0:T(8,128)(2,1)} %gate.1, bf16[1024,896]{1,0:T(8,128)(2,1)} %up.1), custom_call_target="tpu_custom_call" | custom-call | tf_op jit(solution)/shard_map/handover/pallas_call | solution.py:362
  143.3 4.1 %place.1 = (f32[896,512]{1,0:T(8,128)}, bf16[1024,4096]{1,0:T(8,128)(2,1)}) custom-call(f32[896,512]{1,0:T(8,128)S(1)} %get-tuple-element.4.nm, bf16[4,2,1024,512]{3,2,1,0:T(8,128)(2,1)S(1)} %get-tuple-element.5.out), custom_call_target="tpu_custom_call" | custom-call | tf_op jit(solution)/shard_map/place/pallas_call | solution.py:399

commit v3 on v2

--- a/solution.py
+++ b/solution.py
@@ -37,19 +37,32 @@
 
 def plan():
     return [
-        ("X1", 2), ("R", 3), ("HID",), ("X1", 3), ("H", 0), ("H", 4), ("H", 2), ("R", 2), ("X2", 2), ("X2", 3),
-        ("H", 6), ("X1", 1), ("X3", 2), ("X3", 3), ("H", 1), ("H", 3), ("H", 5), ("Y1", 2), ("Y1", 3),
-        ("A2", 2), ("A2", 3), ("R", 1), ("X2", 1), ("X1", 0), ("H", 7), ("M", 2, 0), ("M", 3, 0), ("Z0", 2, 0),
-        ("Z0", 3, 0), ("M", 2, 1), ("R", 0), ("Z2", 2, 0), ("X3", 1), ("Z2", 3, 0), ("Z0", 2, 1), ("M", 3, 1),
-        ("Z3", 2, 0), ("Z2", 2, 1), ("Z3", 3, 0), ("X2", 0), ("Z0", 3, 1), ("Z3", 2, 1), ("Y2", 2, 0),
-        ("Y1", 1), ("Y2", 3, 0), ("X3", 0), ("Z2", 3, 1), ("Y2", 2, 1), ("O2", 2, 0), ("O2", 3, 0), ("A2", 1),
-        ("Z3", 3, 1), ("Y1", 0), ("O2", 2, 1), ("M", 1, 0), ("Y2", 3, 1), ("M", 1, 1), ("Z0", 1, 0), ("A2", 0),
-        ("Z0", 1, 1), ("O2", 3, 1), ("M", 0, 0), ("Z2", 1, 0), ("Z2", 1, 1), ("M", 0, 1), ("Z0", 0, 0),
-        ("Z3", 1, 0), ("O3", 3, 1), ("Z0", 0, 1), ("Z3", 1, 1), ("E", 3, 1), ("Z2", 0, 0), ("Z2", 0, 1),
-        ("O3", 2, 0), ("O3", 2, 1), ("Y2", 1, 0), ("Z3", 0, 0), ("Y2", 1, 1), ("Z3", 0, 1), ("O2", 1, 0),
-        ("Y2", 0, 0), ("O3", 3, 0), ("E", 2, 0), ("Y2", 0, 1), ("O2", 1, 1), ("O3", 1, 0), ("E", 2, 1),
-        ("O2", 0, 0), ("E", 3, 0), ("O2", 0, 1), ("O3", 1, 1), ("O3", 0, 0), ("O3", 0, 1), ("E", 0, 0),
-        ("E", 1, 0), ("E", 1, 1), ("E", 0, 1),
+        ("X1", 0), ("R", 0), ("HID",), ("H", 7), ("H", 1), ("H", 3), ("X2", 0), ("X1", 1), ("X3", 0), ("H", 0),
+        ("R", 1), ("X2", 1), ("Y1", 0), ("H", 4), ("X1", 2), ("X3", 1), ("H", 5), ("A2", 0), ("M", 0, 0, 0),
+        ("Z0", 0, 0, 0), ("Y1", 1), ("R", 2), ("H", 2), ("H", 6), ("Z2", 0, 0, 0), ("M", 0, 0, 1),
+        ("Z0", 0, 0, 1), ("A2", 1), ("X2", 2), ("M", 1, 0, 0), ("Z0", 1, 0, 0), ("Z3", 0, 0, 0),
+        ("Z2", 0, 0, 1), ("X1", 3), ("R", 3), ("M", 0, 1, 1), ("M", 1, 1, 0), ("Z2", 1, 0, 0), ("Z0", 0, 1, 1),
+        ("M", 1, 1, 1), ("Y2", 0, 0, 0), ("Z3", 0, 0, 1), ("Z0", 1, 1, 0), ("M", 0, 1, 0), ("Z3", 1, 0, 0),
+        ("Z2", 0, 1, 1), ("Z0", 1, 1, 1), ("X3", 2), ("Z0", 0, 1, 0), ("M", 1, 0, 1), ("Z2", 1, 1, 0),
+        ("Z2", 1, 1, 1), ("Z0", 1, 0, 1), ("Z3", 0, 1, 1), ("X2", 3), ("Z2", 0, 1, 0), ("Y2", 0, 0, 1),
+        ("Z3", 1, 1, 1), ("Z2", 1, 0, 1), ("Z3", 1, 1, 0), ("Y2", 1, 0, 0), ("Y1", 2), ("Y2", 0, 1, 1),
+        ("O2", 0, 0, 0), ("Z3", 0, 1, 0), ("Y2", 1, 1, 1), ("Z3", 1, 0, 1), ("Y2", 1, 1, 0), ("X3", 3),
+        ("O2", 0, 1, 1), ("O2", 0, 0, 1), ("Y2", 0, 1, 0), ("Y2", 1, 0, 1), ("O2", 1, 1, 1), ("O2", 1, 0, 0),
+        ("O2", 1, 1, 0), ("A2", 2), ("M", 2, 0, 0), ("M", 2, 1, 0), ("Z0", 2, 0, 0), ("Y1", 3), ("O2", 0, 1, 0),
+        ("O2", 1, 0, 1), ("Z0", 2, 1, 0), ("M", 2, 1, 1), ("Z2", 2, 0, 0), ("M", 2, 0, 1), ("Z0", 2, 1, 1),
+        ("Z0", 2, 0, 1), ("Z2", 2, 1, 0), ("Z3", 2, 0, 0), ("A2", 3), ("M", 3, 1, 0), ("Z2", 2, 1, 1),
+        ("Z2", 2, 0, 1), ("M", 3, 0, 0), ("Z0", 3, 1, 0), ("O3", 1, 0, 1), ("Z3", 2, 1, 0), ("Z0", 3, 0, 0),
+        ("Y2", 2, 0, 0), ("M", 3, 1, 1), ("E", 1, 0, 1), ("Z2", 3, 1, 0), ("M", 3, 0, 1), ("Z2", 3, 0, 0),
+        ("Z0", 3, 1, 1), ("Z3", 2, 0, 1), ("Z0", 3, 0, 1), ("Z3", 2, 1, 1), ("O2", 2, 0, 0), ("O3", 0, 0, 0),
+        ("O3", 1, 1, 1), ("O3", 1, 1, 0), ("Z3", 3, 1, 0), ("Z2", 3, 1, 1), ("Y2", 2, 1, 0), ("Z3", 3, 0, 0),
+        ("Z2", 3, 0, 1), ("Y2", 2, 1, 1), ("O3", 1, 0, 0), ("Y2", 3, 1, 0), ("Z3", 3, 1, 1), ("Y2", 2, 0, 1),
+        ("O3", 0, 1, 1), ("Z3", 3, 0, 1), ("Y2", 3, 0, 0), ("O2", 3, 1, 0), ("O3", 0, 0, 1), ("Y2", 3, 1, 1),
+        ("O3", 0, 1, 0), ("E", 0, 0, 0), ("O2", 2, 0, 1), ("Y2", 3, 0, 1), ("E", 1, 1, 0), ("E", 1, 0, 0),
+        ("O2", 3, 0, 0), ("O2", 2, 1, 0), ("O3", 2, 0, 0), ("O2", 3, 1, 1), ("O3", 2, 0, 1), ("O3", 3, 1, 0),
+        ("E", 2, 0, 0), ("O2", 2, 1, 1), ("E", 0, 1, 1), ("O2", 3, 0, 1), ("O3", 3, 0, 0), ("E", 0, 0, 1),
+        ("O3", 2, 1, 0), ("E", 3, 1, 0), ("O3", 3, 1, 1), ("O3", 2, 1, 1), ("E", 2, 0, 1), ("O3", 3, 0, 1),
+        ("E", 2, 1, 1), ("E", 3, 1, 1), ("E", 1, 1, 1), ("E", 2, 1, 0), ("E", 3, 0, 0), ("E", 0, 1, 0),
+        ("E", 3, 0, 1),
     ]
 
 
@@ -83,13 +96,19 @@
     rows = gown.shape[1]
     half = rows // 2
     tokens = hid.shape[1]
-    wide = p.shape[3]
     core_rows = tokens // 2
     zrows = core_rows // 4
     zh = zrows // 2
 
     sends = []
     done = {}
+    seen = set()
+
+    def arrive(*keys):
+        for key in keys:
+            if key not in seen:
+                seen.add(key)
+                done[key].wait_recv()
 
     def remote(src, dst, s, r, to):
         cp = pltpu.make_async_remote_copy(
@@ -199,19 +218,19 @@
             old = mst_v[at, cols]
             new = old - learn_rate * (update + weight_decay * old)
             mst_v[at, cols] = new
-            w[k, x, at, :] = new.astype(BF16)
+            w[k, 0, at, :] = new.astype(BF16)
 
         sweep(rows, 64, body)
         for d in (0, 1):
             done["a1", d, k] = remote(
-                w.at[k, x], w.at[k, x], a1s.at[d, k], a1r.at[d, k], X[d])
+                w.at[k, 0], w.at[k, 2 - d], a1s.at[d, k], a1r.at[d, k], X[d])
 
     def A2(k):
-        for d, origin in ((0, xp), (1, xn)):
-            done["a1", d, k].wait_recv()
+        for d in (0, 1):
+            arrive(("a1", d, k))
             at = pl.ds(d * half, half)
             done["a2", d, k] = remote(
-                w.at[k, origin, at], w.at[k, origin, at], a2s.at[d, k], a2r.at[d, k], X[d])
+                w.at[k, 2 - d, at], w.at[k, 3, at], a2s.at[d, k], a2r.at[d, k], X[d])
 
     piece = tokens // HP
 
@@ -229,102 +248,92 @@
         at = pl.ds(i * piece, piece)
         done["h", i] = remote(hid.at[0, at], hid.at[1, at], hs.at[i], hr.at[i], YL)
 
-    def M(k, h):
-        if h == 0:
-            for d in (0, 1):
-                done["a2", d, k].wait_recv()
-        elif ("h", 0) in done:
-            for i in range(HP):
-                done.pop(("h", i)).wait_recv()
+    def M(k, h, q):
+        arrive(("a1", 0, k), ("a1", 1, k))
+        if q == 1:
+            arrive(("a2", 0, k), ("a2", 1, k))
+        if h == 1:
+            arrive(*(("h", i) for i in range(HP)))
         for part in (1 - c, c):
-            def body(r):
-                at = pl.ds(pl.multiple_of(part * core_rows + r, 256), 256)
-                weights = jnp.concatenate([w[k, j] for j in range(4)], axis=1)
-                p[k, h, at, :] = jnp.dot(
-                    hid[h, at, :], weights, preferred_element_type=F32).astype(BF16)
-
-            sweep(core_rows, 256, body)
+            at = pl.ds(pl.multiple_of(part * core_rows, core_rows), core_rows)
+            weights = jnp.concatenate([w[k, 2 * q], w[k, 2 * q + 1]], axis=1)
+            p[k, h, q, at, :] = jnp.dot(
+                hid[h, at, :], weights, preferred_element_type=F32).astype(BF16)
             if part is not c:
-                at = pl.ds(pl.multiple_of((1 - c) * core_rows, core_rows), core_rows)
-                done["c", k, h] = remote(p.at[k, h, at], rc.at[k, h], cs.at[k, h], cr.at[k, h], C)
+                done["c", k, h, q] = remote(p.at[k, h, q, at], rc.at[k, h, q], cs.at[k, h, q], cr.at[k, h, q], C)
 
     base = c * core_rows
 
     def zat(owner, part, count):
         return pl.ds(pl.multiple_of(base + owner * zrows + part * zh, zh), count)
 
-    def Z0(k, h):
-        done["c", k, h].wait_recv()
+    def Z0(k, h, q):
+        arrive(("c", k, h, q))
 
         def body(r):
-            at = pl.ds(pl.multiple_of(base + r, 64), 64)
-            p[k, h, at, :] = (p[k, h, at, :].astype(F32) + rc[k, h, pl.ds(r, 64), :].astype(F32)).astype(BF16)
-
-        sweep(core_rows, 64, body)
-        for d in (0, 1):
-            done["z1", d, k, h] = remote(
-                p.at[k, h, zat(zo, d, zh)], zr1.at[d, k, h], z1s.at[d, k, h], z1r.at[d, k, h], Z[d])
+            at = pl.ds(pl.multiple_of(base + r, 128), 128)
+            p[k, h, q, at, :] = (
+                p[k, h, q, at, :].astype(F32) + rc[k, h, q, pl.ds(r, 128), :].astype(F32)).astype(BF16)
+
+        sweep(core_rows, 128, body)
+        for d in (0, 1):
+            done["z1", d, k, h, q] = remote(
+                p.at[k, h, q, zat(zo, d, zh)], zr1.at[d, k, h, q], z1s.at[d, k, h, q], z1r.at[d, k, h, q], Z[d])
         for d, owner in ((0, zn), (1, zp)):
-            done["zw", d, k, h] = remote(
-                p.at[k, h, zat(owner, 1 - d, zh)], zr2.at[d, k, h, pl.ds((1 - d) * zh, zh)],
-                zws.at[d, k, h], zwr.at[d, k, h], Z[d])
-
-    def Z2(k, h):
+            done["zw", d, k, h, q] = remote(
+                p.at[k, h, q, zat(owner, 1 - d, zh)], zr2.at[d, k, h, q, pl.ds((1 - d) * zh, zh)],
+                zws.at[d, k, h, q], zwr.at[d, k, h, q], Z[d])
+
+    def Z2(k, h, q):
         for d, owner in ((0, zn), (1, zp)):
-            done["z1", d, k, h].wait_recv()
+            arrive(("z1", d, k, h, q))
             at = zat(owner, d, zh)
-            p[k, h, at, :] = (p[k, h, at, :].astype(F32) + zr1[d, k, h].astype(F32)).astype(BF16)
-            done["z2", d, k, h] = remote(
-                p.at[k, h, at], zr2.at[d, k, h, pl.ds(d * zh, zh)], z2s.at[d, k, h], z2r.at[d, k, h], Z[d])
-
-    def Z3(k, h):
-        for d in (0, 1):
-            done["zw", d, k, h].wait_recv()
-            done["z2", d, k, h].wait_recv()
+            p[k, h, q, at, :] = (p[k, h, q, at, :].astype(F32) + zr1[d, k, h, q].astype(F32)).astype(BF16)
+            done["z2", d, k, h, q] = remote(
+                p.at[k, h, q, at], zr2.at[d, k, h, q, pl.ds(d * zh, zh)], z2s.at[d, k, h, q], z2r.at[d, k, h, q], Z[d])
+
+    def Z3(k, h, q):
+        for d in (0, 1):
+            arrive(("zw", d, k, h, q), ("z2", d, k, h, q))
         for part in (0, 1):
             at = pl.ds(part * zh, zh)
-            yb[k, h, at, :] = (
-                p[k, h, zat(z, part, zh), :].astype(F32)
-                + zr2[0, k, h, at, :].astype(F32)
-                + zr2[1, k, h, at, :].astype(F32)
+            yb[k, h, q, at, :] = (
+                p[k, h, q, zat(z, part, zh), :].astype(F32)
+                + zr2[0, k, h, q, at, :].astype(F32)
+                + zr2[1, k, h, q, at, :].astype(F32)
             ).astype(BF16)
         for i, to in ((0, YH),) if h == 0 else ((1, YL), (2, YD)):
-            done["y3", k, i] = remote(yb.at[k, h], yr.at[k, i], y3s.at[k, i], y3r.at[k, i], to)
-
-    def oat(owner, part, count):
-        return pl.ds(pl.multiple_of(base + owner * zrows + part * zh, zh), count)
-
-    def Y2(k, h):
+            done["y3", i, k, q] = remote(yb.at[k, h, q], yr.at[i, k, q], y3s.at[i, k, q], y3r.at[i, k, q], to)
+
+    def Y2(k, h, q):
         group = yl if h == 0 else 1 - yl
-        for i in (0,) if h == 0 else (1, 2):
-            done["y3", k, i].wait_recv()
+        arrive(*(("y3", i, k, q) for i in ((0,) if h == 0 else (1, 2))))
         for part in (0, 1):
             at = pl.ds(part * zh, zh)
             if h == 0:
-                total = yb[k, 0, at, :].astype(F32) + yr[k, 0, at, :].astype(F32)
+                total = yb[k, 0, q, at, :].astype(F32) + yr[0, k, q, at, :].astype(F32)
             else:
-                total = yr[k, 1, at, :].astype(F32) + yr[k, 2, at, :].astype(F32)
-            out[k, group, oat(z, part, zh), :] = total.astype(BF16)
-        mine = out.at[k, group, oat(z, 0, zrows)]
-        for d in (0, 1):
-            done["o1", d, k, h] = remote(mine, mine, o1s.at[d, k, h], o1r.at[d, k, h], Z[d])
-
-    def O2(k, h):
+                total = yr[1, k, q, at, :].astype(F32) + yr[2, k, q, at, :].astype(F32)
+            out[k, group, q, zat(z, part, zh), :] = total.astype(BF16)
+        mine = out.at[k, group, q, zat(z, 0, zrows)]
+        for d in (0, 1):
+            done["o1", d, k, h, q] = remote(mine, mine, o1s.at[d, k, h, q], o1r.at[d, k, h, q], Z[d])
+
+    def O2(k, h, q):
         group = yl if h == 0 else 1 - yl
         for d, origin in ((0, zp), (1, zn)):
-            done["o1", d, k, h].wait_recv()
-            part = out.at[k, group, oat(origin, d, zh)]
-            done["o2", d, k, h] = remote(part, part, o2s.at[d, k, h], o2r.at[d, k, h], Z[d])
-
-    def O3(k, h):
+            arrive(("o1", d, k, h, q))
+            part = out.at[k, group, q, zat(origin, d, zh)]
+            done["o2", d, k, h, q] = remote(part, part, o2s.at[d, k, h, q], o2r.at[d, k, h, q], Z[d])
+
+    def O3(k, h, q):
         group = yl if h == 0 else 1 - yl
-        for d in (0, 1):
-            done["o2", d, k, h].wait_recv()
-        part = out.at[k, group, pl.ds(pl.multiple_of(base, core_rows), core_rows)]
-        done["oc", k, h] = remote(part, part, ocs.at[k, h], ocr.at[k, h], C)
-
-    def E(k, h):
-        done["oc", k, h].wait_recv()
+        arrive(("o2", 0, k, h, q), ("o2", 1, k, h, q))
+        part = out.at[k, group, q, pl.ds(pl.multiple_of(base, core_rows), core_rows)]
+        done["oc", k, h, q] = remote(part, part, ocs.at[k, h, q], ocr.at[k, h, q], C)
+
+    def E(k, h, q):
+        arrive(("oc", k, h, q))
 
     steps = dict(X1=X1, R=R, X2=X2, X3=X3, Y1=Y1, A2=A2, HID=HID, H=H, M=M, Z0=Z0, Z2=Z2, Z3=Z3, Y2=Y2, O2=O2, O3=O3, E=E)
     for name, *at in plan():
@@ -335,13 +344,16 @@
 
 
 def place(nm, out, nm_out, mix_out, sems):
+    x = lax.div(lax.axis_index("dp"), 2)
     copies = [pltpu.make_async_copy(nm, nm_out, sems.at[0])]
     for k in range(K):
         for group in (0, 1):
-            for j in range(4):
-                at = pl.ds((j * 2 * K + group * K + k) * LANES, LANES)
+            for slot, ahead in enumerate((0, 1, 3, 2)):
+                owner = lax.rem(x + ahead, 4)
+                at = pl.ds(pl.multiple_of((owner * 2 * K + group * K + k) * LANES, LANES), LANES)
                 copies.append(pltpu.make_async_copy(
-                    out.at[k, group, :, pl.ds(j * LANES, LANES)], mix_out.at[:, at], sems.at[len(copies)]))
+                    out.at[k, group, slot // 2, :, pl.ds(slot % 2 * LANES, LANES)],
+                    mix_out.at[:, at], sems.at[len(copies)]))
     for cp in copies:
         cp.start()
     for cp in copies:
@@ -363,7 +375,7 @@
         kernel,
         out_shape=(
             vm(master.shape, F32),
-            vm((K, 2, tokens, block), BF16),
+            vm((K, 2, 2, tokens, block // 2), BF16),
         ),
         in_specs=[hbm] * 6,
         scratch_shapes=[
@@ -379,17 +391,17 @@
             vm((tokens, rows), BF16),
             vm((tokens, rows), BF16),
             vm((2, tokens, rows), BF16),
-            vm((K, 2, tokens, block), BF16),
-            vm((K, 2, tokens // 2, block), BF16),
-            vm((2, K, 2, tokens // 16, block), BF16),
-            vm((2, K, 2, tokens // 8, block), BF16),
-            vm((K, 2, tokens // 8, block), BF16),
-            vm((K, 3, tokens // 8, block), BF16),
+            vm((K, 2, 2, tokens, block // 2), BF16),
+            vm((K, 2, 2, tokens // 2, block // 2), BF16),
+            vm((2, K, 2, 2, tokens // 16, block // 2), BF16),
+            vm((2, K, 2, 2, tokens // 8, block // 2), BF16),
+            vm((K, 2, 2, tokens // 8, block // 2), BF16),
+            vm((3, K, 2, tokens // 8, block // 2), BF16),
             dma((9,)),
             *pair((2, K)), *pair((2, K)), *pair((2, K)), *pair((K,)),
             *pair((2, K)), *pair((2, K)), *pair((HP,)),
-            *pair((K, 2)), *pair((2, K, 2)), *pair((2, K, 2)), *pair((2, K, 2)),
-            *pair((K, 3)), *pair((2, K, 2)), *pair((2, K, 2)), *pair((K, 2)),
+            *pair((K, 2, 2)), *pair((2, K, 2, 2)), *pair((2, K, 2, 2)), *pair((2, K, 2, 2)),
+            *pair((3, K, 2)), *pair((2, K, 2, 2)), *pair((2, K, 2, 2)), *pair((K, 2, 2)),
         ],
         compiler_params=pltpu.CompilerParams(
             collective_id=0, has_side_effects=True, vmem_limit_bytes=50 * 2**20

time: 147 us -> 142 us (0.966)
  Pallas kernels: 147 us -> 142 us
    pallas_call x1, Pallas kernels: 143 us -> 138 us  [per_device(): pl.pallas_call(kernel, out_shape=(vm(master.shape, F32), vm((K, 2, 2, tok...]
where the time goes in v3:
time: 142 us
  Pallas kernels  142 us (100%)
    pallas_call x1, Pallas kernels, per_device(): pl.pallas_call(kernel, out_shape=(vm(master.shape, F32), vm((K, 2, 2, tok...  138 us
    pallas_call x1, Pallas kernels, per_device(): pl.pallas_call(place, out_shape=(jax.ShapeDtypeStruct(master.shape, F32),...  4.1 us

profile of v3, /device:TPU:1, one launch (start us, length us, event | category | flops | bytes accessed | tf_op | source)
XLA Modules:
  0.0 142.3 jit_solution(7013601703270780154)
XLA Ops:
  0.6 137.6 %handover.1 = (f32[896,512]{1,0:T(8,128)S(1)}, bf16[4,2,2,1024,256]{4,3,2,1,0:T(8,128)(2,1)S(1)}) custom-call(bf16[1,896,4096]{2,1,0:T(8,128)(2,1)} %g.1, f32[896,512]{1,0:T(8,128)} %mst.1, f32[896,512]{1,0:T(8,128)} %mom.1, f32[896,512]{1,0:T(8,128)} %sqr.1, bf16[1024,896]{1,0:T(8,128)(2,1)} %gate.1, bf16[1024,896]{1,0:T(8,128)(2,1)} %up.1), custom_call_target="tpu_custom_call" | custom-call | tf_op jit(solution)/shard_map/handover/pallas_call | solution.py:374
  138.2 4.1 %place.1 = (f32[896,512]{1,0:T(8,128)}, bf16[1024,4096]{1,0:T(8,128)(2,1)}) custom-call(f32[896,512]{1,0:T(8,128)S(1)} %get-tuple-element.4.nm, bf16[4,2,2,1024,256]{4,3,2,1,0:T(8,128)(2,1)S(1)} %get-tuple-element.5.out), custom_call_target="tpu_custom_call" | custom-call | tf_op jit(solution)/shard_map/place/pallas_call | solution.py:411

commit v4 on v3

--- a/solution.py
+++ b/solution.py
@@ -23,6 +23,7 @@
 K = 4
 LANES = 128
 HP = 8
+LATER = 6
 
 
 def sweep(rows, tile, body):
@@ -37,41 +38,45 @@
 
 def plan():
     return [
-        ("X1", 0), ("R", 0), ("HID",), ("H", 7), ("H", 1), ("H", 3), ("X2", 0), ("X1", 1), ("X3", 0), ("H", 0),
-        ("R", 1), ("X2", 1), ("Y1", 0), ("H", 4), ("X1", 2), ("X3", 1), ("H", 5), ("A2", 0), ("M", 0, 0, 0),
-        ("Z0", 0, 0, 0), ("Y1", 1), ("R", 2), ("H", 2), ("H", 6), ("Z2", 0, 0, 0), ("M", 0, 0, 1),
-        ("Z0", 0, 0, 1), ("A2", 1), ("X2", 2), ("M", 1, 0, 0), ("Z0", 1, 0, 0), ("Z3", 0, 0, 0),
-        ("Z2", 0, 0, 1), ("X1", 3), ("R", 3), ("M", 0, 1, 1), ("M", 1, 1, 0), ("Z2", 1, 0, 0), ("Z0", 0, 1, 1),
-        ("M", 1, 1, 1), ("Y2", 0, 0, 0), ("Z3", 0, 0, 1), ("Z0", 1, 1, 0), ("M", 0, 1, 0), ("Z3", 1, 0, 0),
-        ("Z2", 0, 1, 1), ("Z0", 1, 1, 1), ("X3", 2), ("Z0", 0, 1, 0), ("M", 1, 0, 1), ("Z2", 1, 1, 0),
-        ("Z2", 1, 1, 1), ("Z0", 1, 0, 1), ("Z3", 0, 1, 1), ("X2", 3), ("Z2", 0, 1, 0), ("Y2", 0, 0, 1),
-        ("Z3", 1, 1, 1), ("Z2", 1, 0, 1), ("Z3", 1, 1, 0), ("Y2", 1, 0, 0), ("Y1", 2), ("Y2", 0, 1, 1),
-        ("O2", 0, 0, 0), ("Z3", 0, 1, 0), ("Y2", 1, 1, 1), ("Z3", 1, 0, 1), ("Y2", 1, 1, 0), ("X3", 3),
-        ("O2", 0, 1, 1), ("O2", 0, 0, 1), ("Y2", 0, 1, 0), ("Y2", 1, 0, 1), ("O2", 1, 1, 1), ("O2", 1, 0, 0),
-        ("O2", 1, 1, 0), ("A2", 2), ("M", 2, 0, 0), ("M", 2, 1, 0), ("Z0", 2, 0, 0), ("Y1", 3), ("O2", 0, 1, 0),
-        ("O2", 1, 0, 1), ("Z0", 2, 1, 0), ("M", 2, 1, 1), ("Z2", 2, 0, 0), ("M", 2, 0, 1), ("Z0", 2, 1, 1),
-        ("Z0", 2, 0, 1), ("Z2", 2, 1, 0), ("Z3", 2, 0, 0), ("A2", 3), ("M", 3, 1, 0), ("Z2", 2, 1, 1),
-        ("Z2", 2, 0, 1), ("M", 3, 0, 0), ("Z0", 3, 1, 0), ("O3", 1, 0, 1), ("Z3", 2, 1, 0), ("Z0", 3, 0, 0),
-        ("Y2", 2, 0, 0), ("M", 3, 1, 1), ("E", 1, 0, 1), ("Z2", 3, 1, 0), ("M", 3, 0, 1), ("Z2", 3, 0, 0),
-        ("Z0", 3, 1, 1), ("Z3", 2, 0, 1), ("Z0", 3, 0, 1), ("Z3", 2, 1, 1), ("O2", 2, 0, 0), ("O3", 0, 0, 0),
-        ("O3", 1, 1, 1), ("O3", 1, 1, 0), ("Z3", 3, 1, 0), ("Z2", 3, 1, 1), ("Y2", 2, 1, 0), ("Z3", 3, 0, 0),
-        ("Z2", 3, 0, 1), ("Y2", 2, 1, 1), ("O3", 1, 0, 0), ("Y2", 3, 1, 0), ("Z3", 3, 1, 1), ("Y2", 2, 0, 1),
-        ("O3", 0, 1, 1), ("Z3", 3, 0, 1), ("Y2", 3, 0, 0), ("O2", 3, 1, 0), ("O3", 0, 0, 1), ("Y2", 3, 1, 1),
-        ("O3", 0, 1, 0), ("E", 0, 0, 0), ("O2", 2, 0, 1), ("Y2", 3, 0, 1), ("E", 1, 1, 0), ("E", 1, 0, 0),
-        ("O2", 3, 0, 0), ("O2", 2, 1, 0), ("O3", 2, 0, 0), ("O2", 3, 1, 1), ("O3", 2, 0, 1), ("O3", 3, 1, 0),
-        ("E", 2, 0, 0), ("O2", 2, 1, 1), ("E", 0, 1, 1), ("O2", 3, 0, 1), ("O3", 3, 0, 0), ("E", 0, 0, 1),
-        ("O3", 2, 1, 0), ("E", 3, 1, 0), ("O3", 3, 1, 1), ("O3", 2, 1, 1), ("E", 2, 0, 1), ("O3", 3, 0, 1),
-        ("E", 2, 1, 1), ("E", 3, 1, 1), ("E", 1, 1, 1), ("E", 2, 1, 0), ("E", 3, 0, 0), ("E", 0, 1, 0),
-        ("E", 3, 0, 1),
+        ("X1", 1), ("HID", 6), ("H", 6), ("HID", 4), ("HID", 2), ("L", 1), ("H", 4), ("HID", 3), ("R", 1),
+        ("L", 0), ("X1", 2), ("X2", 1, 0), ("H", 3), ("HID", 1), ("L", 2), ("X2", 1, 1), ("HID", 5), ("R", 2),
+        ("H", 2), ("HID", 7), ("X3", 1, 0), ("X2", 2, 0), ("X2", 2, 1), ("X3", 1, 1), ("H", 7), ("Y1", 1, 1),
+        ("X3", 2, 0), ("HID", 0), ("Y1", 1, 0), ("X1", 0), ("X3", 2, 1), ("H", 0), ("M", 1, 0, 0), ("A2", 1, 0),
+        ("A2", 1, 1), ("H", 1), ("Y1", 2, 0), ("Y1", 2, 1), ("Z0", 1, 0, 0), ("R", 0), ("H", 5), ("X2", 0, 0),
+        ("Z2", 1, 0, 0), ("M", 1, 0, 1), ("X2", 0, 1), ("Z3", 1, 0, 0), ("Z0", 1, 0, 1), ("A2", 2, 0),
+        ("M", 2, 0, 0), ("Z2", 1, 0, 1), ("A2", 2, 1), ("X1", 3), ("Z0", 2, 0, 0), ("M", 1, 1, 1),
+        ("Z3", 1, 0, 1), ("Y2", 1, 0, 0), ("M", 2, 1, 0), ("Z2", 2, 0, 0), ("Z0", 1, 1, 1), ("X3", 0, 0),
+        ("Z0", 2, 1, 0), ("M", 1, 1, 0), ("X3", 0, 1), ("Y2", 1, 0, 1), ("Z3", 2, 0, 0), ("Z0", 1, 1, 0),
+        ("Z2", 1, 1, 1), ("O2", 1, 0, 0), ("Z2", 2, 1, 0), ("M", 2, 0, 1), ("Y1", 0, 0), ("O2", 1, 0, 1),
+        ("M", 2, 1, 1), ("Z2", 1, 1, 0), ("Y1", 0, 1), ("Z0", 2, 0, 1), ("O3", 1, 0, 0), ("Z3", 1, 1, 1),
+        ("R", 3), ("Z0", 2, 1, 1), ("X2", 3, 1), ("Z3", 2, 1, 0), ("Y2", 2, 0, 0), ("Z3", 1, 1, 0),
+        ("X2", 3, 0), ("Z2", 2, 0, 1), ("Y2", 1, 1, 1), ("A2", 0, 1), ("Z2", 2, 1, 1), ("M", 0, 0, 0),
+        ("Y2", 2, 1, 0), ("M", 0, 1, 0), ("Z0", 0, 0, 0), ("Z3", 2, 0, 1), ("A2", 0, 0), ("Z0", 0, 1, 0),
+        ("Z3", 2, 1, 1), ("Y2", 1, 1, 0), ("Z2", 0, 0, 0), ("X3", 3, 1), ("Z2", 0, 1, 0), ("Y2", 2, 0, 1),
+        ("Y2", 2, 1, 1), ("O2", 1, 1, 1), ("X3", 3, 0), ("Z3", 0, 0, 0), ("O2", 2, 1, 0), ("O2", 2, 0, 0),
+        ("Z3", 0, 1, 0), ("O2", 1, 1, 0), ("Y1", 3, 1), ("M", 0, 0, 1), ("O2", 2, 1, 1), ("O2", 2, 0, 1),
+        ("Y1", 3, 0), ("Z0", 0, 0, 1), ("M", 0, 1, 1), ("Y2", 0, 0, 0), ("Y2", 0, 1, 0), ("A2", 3, 1),
+        ("Z0", 0, 1, 1), ("Z2", 0, 0, 1), ("O3", 2, 0, 0), ("A2", 3, 0), ("M", 3, 0, 0), ("O2", 0, 0, 0),
+        ("M", 3, 1, 0), ("Z0", 3, 0, 0), ("O2", 0, 1, 0), ("Z2", 0, 1, 1), ("Z0", 3, 1, 0), ("Z3", 0, 0, 1),
+        ("M", 3, 0, 1), ("Z2", 3, 0, 0), ("M", 3, 1, 1), ("Z0", 3, 0, 1), ("O3", 1, 1, 0), ("E", 2, 0, 0),
+        ("O3", 2, 1, 1), ("Z3", 0, 1, 1), ("Z2", 3, 1, 0), ("Z0", 3, 1, 1), ("Z3", 3, 0, 0), ("Z2", 3, 0, 1),
+        ("Y2", 0, 0, 1), ("Z3", 3, 1, 0), ("E", 1, 0, 0), ("Z2", 3, 1, 1), ("Y2", 0, 1, 1), ("Z3", 3, 0, 1),
+        ("E", 2, 1, 1), ("O3", 2, 1, 0), ("Y2", 3, 0, 0), ("Z3", 3, 1, 1), ("O3", 1, 0, 1), ("Y2", 3, 1, 0),
+        ("O2", 0, 1, 1), ("E", 1, 0, 1), ("Y2", 3, 0, 1), ("O3", 0, 1, 0), ("O3", 1, 1, 1), ("Y2", 3, 1, 1),
+        ("O2", 0, 0, 1), ("O2", 3, 0, 0), ("O3", 0, 0, 0), ("E", 2, 1, 0), ("O2", 3, 1, 0), ("O3", 0, 1, 1),
+        ("O2", 3, 0, 1), ("O2", 3, 1, 1), ("O3", 2, 0, 1), ("O3", 0, 0, 1), ("E", 0, 1, 1), ("O3", 3, 0, 0),
+        ("E", 1, 1, 0), ("O3", 3, 1, 0), ("E", 2, 0, 1), ("E", 0, 0, 0), ("E", 0, 1, 0), ("O3", 3, 0, 1),
+        ("O3", 3, 1, 1), ("E", 0, 0, 1), ("E", 3, 1, 0), ("E", 3, 0, 0), ("E", 1, 1, 1), ("E", 3, 0, 1),
+        ("E", 3, 1, 1),
     ]
 
 
 def kernel(
     g, mst, mom, sqr, gate, up,
     mst_v, out,
-    gown, gfw, r1, r2, sy, ry, mom_v, sqr_v, w, gate_v, up_v, hid,
+    gv, r1, r2, sy, ry, mom_v, sqr_v, w, gate_v, up_v, hid,
     p, rc, zr1, zr2, yb, yr,
-    ld,
+    lg, ld,
     x1s, x1r, rws, rwr, x2s, x2r, ys, yrs, a1s, a1r, a2s, a2r, hs, hr,
     cs, cr, z1s, z1r, zws, zwr, z2s, z2r, y3s, y3r, o1s, o1r, o2s, o2r, ocs, ocr,
 ):
@@ -93,56 +98,70 @@
     YD = dev(yl=1 - yl, yh=1 - yh)
     C = dev(c=1 - c)
 
-    rows = gown.shape[1]
+    rows = gv.shape[3]
     half = rows // 2
     tokens = hid.shape[1]
     core_rows = tokens // 2
     zrows = core_rows // 4
     zh = zrows // 2
 
-    sends = []
     done = {}
     seen = set()
+    settled = []
+    step_at = [0]
 
     def arrive(*keys):
         for key in keys:
             if key not in seen:
                 seen.add(key)
                 done[key].wait_recv()
+                settled.append((step_at[0], done[key]))
 
     def remote(src, dst, s, r, to):
         cp = pltpu.make_async_remote_copy(
             src_ref=src, dst_ref=dst, send_sem=s, recv_sem=r, device_id=to, device_id_type=MESH
         )
         cp.start()
-        sends.append(cp)
         return cp
 
     def columns(owner, strip, k, width=LANES):
         return pl.ds(pl.multiple_of(owner * (2 * K * LANES) + strip * (K * LANES) + k * LANES, LANES), width)
 
     loads = {}
-
-    def load(name, i, src, dst):
-        cp = pltpu.make_async_copy(src, dst, ld.at[i])
+    ready = set()
+
+    def load(name, sem, src, dst):
+        cp = pltpu.make_async_copy(src, dst, sem)
         cp.start()
         loads[name] = cp
 
-    block = K * LANES
-    load("f0", 0, g.at[0, :, columns(xn, 0, 0, block)], gfw.at[0])
-    load("f1", 1, g.at[0, :, columns(xp, 1, 0, block)], gfw.at[1])
-    load("gate", 2, gate, gate_v)
-    load("up", 3, up, up_v)
-    load("own0", 4, g.at[0, :, columns(x, 0, 0, block)], gown.at[0])
-    load("own1", 5, g.at[0, :, columns(x, 1, 0, block)], gown.at[1])
-    load("mst", 6, mst, mst_v)
-    load("mom", 7, mom, mom_v)
-    load("sqr", 8, sqr, sqr_v)
-
     def loaded(*names):
         for n in names:
-            if n in loads:
+            if n not in ready:
+                ready.add(n)
                 loads.pop(n).wait()
+
+    owners = (x, xn, xo, xp)
+
+    def loadg(k):
+        for o, strip in ((2, 0), (2, 1), (1, 1), (3, 0), (1, 0), (3, 1), (0, 0), (0, 1)):
+            load(("g", o, strip, k), lg.at[o, strip, k], g.at[0, :, columns(owners[o], strip, k)], gv.at[o, strip, k])
+
+    chunks = [step[1] for step in plan() if step[0] == "X1"]
+    loadg(chunks[0])
+    load("gate", ld.at[0], gate, gate_v)
+    load("up", ld.at[1], up, up_v)
+
+    def L(i):
+        if i == 0:
+            loadg(chunks[1])
+        elif i == 1:
+            loadg(chunks[2])
+            loadg(chunks[3])
+        else:
+            load("mst", ld.at[2], mst, mst_v)
+            load("mom", ld.at[3], mom, mom_v)
+            load("sqr", ld.at[4], sqr, sqr_v)
 
     barrier = pltpu.get_barrier_semaphore()
     friends = (*X, *Z, YL, YH, YD, C)
@@ -151,63 +170,61 @@
     pl.semaphore_wait(barrier, len(friends))
 
     def X1(k):
-        done["x1", 0, k] = remote(
-            g.at[0, :, columns(xo, 0, k)], r1.at[0, k], x1s.at[0, k], x1r.at[0, k], X[0])
-        done["x1", 1, k] = remote(
-            g.at[0, :, columns(xo, 1, k)], r1.at[1, k], x1s.at[1, k], x1r.at[1, k], X[1])
+        for d in (0, 1):
+            loaded(("g", 2, d, k))
+            done["x1", d, k] = remote(gv.at[2, d, k], r1.at[d, k], x1s.at[d, k], x1r.at[d, k], X[d])
 
     def R(k):
-        done["rw", 0, k] = remote(
-            g.at[0, :, columns(xn, 1, k)], r2.at[0, k, 1], rws.at[0, k], rwr.at[0, k], X[0])
-        done["rw", 1, k] = remote(
-            g.at[0, :, columns(xp, 0, k)], r2.at[1, k, 0], rws.at[1, k], rwr.at[1, k], X[1])
-
-    def X2(k):
-        loaded("f0", "f1")
-        cols = pl.ds(k * LANES, LANES)
-        for d in (0, 1):
-            done["x1", d, k].wait_recv()
+        for d, o in ((0, 1), (1, 3)):
+            loaded(("g", o, 1 - d, k))
+            done["rw", d, k] = remote(
+                gv.at[o, 1 - d, k], r2.at[d, k, 1 - d], rws.at[d, k], rwr.at[d, k], X[d])
+
+    def X2(k, part):
+        at_part = pl.ds(part * half, half)
+        for d, o in ((0, 1), (1, 3)):
+            loaded(("g", o, d, k))
+            arrive(("x1", d, k))
 
             def body(r):
-                at = pl.ds(r, 128)
-                gfw[d, at, cols] = (gfw[d, at, cols].astype(F32) + r1[d, k, at, :].astype(F32)).astype(BF16)
-
-            sweep(rows, 128, body)
-            done["x2", d, k] = remote(
-                gfw.at[d, :, cols], r2.at[d, k, d], x2s.at[d, k], x2r.at[d, k], X[d])
-
-    def X3(k):
-        loaded("own0", "own1")
-        for d in (0, 1):
-            done["rw", d, k].wait_recv()
-            done["x2", d, k].wait_recv()
-        cols = pl.ds(k * LANES, LANES)
+                at = pl.ds(pl.multiple_of(part * half + r, 64), 64)
+                gv[o, d, k, at, :] = (gv[o, d, k, at, :].astype(F32) + r1[d, k, at, :].astype(F32)).astype(BF16)
+
+            sweep(half, 64, body)
+            done["x2", d, k, part] = remote(
+                gv.at[o, d, k, at_part], r2.at[d, k, d, at_part], x2s.at[d, k, part], x2r.at[d, k, part], X[d])
+
+    def X3(k, part):
+        loaded(("g", 0, 0, k), ("g", 0, 1, k))
+        for d in (0, 1):
+            arrive(("rw", d, k), ("x2", d, k, part))
         other = 1 - yl
 
         def body(r):
-            at = pl.ds(r, 128)
+            at = pl.ds(pl.multiple_of(part * half + r, 64), 64)
             sy[k, at, :] = (
-                gown[other, at, cols].astype(F32)
+                gv[0, other, k, at, :].astype(F32)
                 + r2[0, k, other, at, :].astype(F32)
                 + r2[1, k, other, at, :].astype(F32)
             ).astype(BF16)
 
-        sweep(rows, 128, body)
-        done["y", k] = remote(sy.at[k], ry.at[k], ys.at[k], yrs.at[k], YL)
+        sweep(half, 64, body)
+        at_part = pl.ds(part * half, half)
+        done["y", k, part] = remote(sy.at[k, at_part], ry.at[k, at_part], ys.at[k, part], yrs.at[k, part], YL)
 
     learn_rate = 0.8 / math.sqrt(FF)
     corr_one = 1.0 - beta_one**step_count
     corr_two = 1.0 - beta_two**step_count
 
-    def Y1(k):
+    def Y1(k, part):
         loaded("mst", "mom", "sqr")
-        done["y", k].wait_recv()
+        arrive(("y", k, part))
         cols = pl.ds(k * LANES, LANES)
 
         def body(r):
-            at = pl.ds(r, 64)
+            at = pl.ds(pl.multiple_of(part * half + r, 64), 64)
             grad = (
-                gown[yl, at, cols].astype(F32)
+                gv[0, yl, k, at, :].astype(F32)
                 + r2[0, k, yl, at, :].astype(F32)
                 + r2[1, k, yl, at, :].astype(F32)
                 + ry[k, at, :].astype(F32)
@@ -220,36 +237,36 @@
             mst_v[at, cols] = new
             w[k, 0, at, :] = new.astype(BF16)
 
-        sweep(rows, 64, body)
-        for d in (0, 1):
-            done["a1", d, k] = remote(
-                w.at[k, 0], w.at[k, 2 - d], a1s.at[d, k], a1r.at[d, k], X[d])
-
-    def A2(k):
-        for d in (0, 1):
-            arrive(("a1", d, k))
-            at = pl.ds(d * half, half)
-            done["a2", d, k] = remote(
-                w.at[k, 2 - d, at], w.at[k, 3, at], a2s.at[d, k], a2r.at[d, k], X[d])
+        sweep(half, 64, body)
+        at_part = pl.ds(part * half, half)
+        for d in (0, 1):
+            done["a1", d, k, part] = remote(
+                w.at[k, 0, at_part], w.at[k, 2 - d, at_part], a1s.at[d, k, part], a1r.at[d, k, part], X[d])
+
+    def A2(k, d):
+        arrive(("a1", d, k, d))
+        at = pl.ds(d * half, half)
+        done["a2", d, k] = remote(
+            w.at[k, 2 - d, at], w.at[k, 3, at], a2s.at[d, k], a2r.at[d, k], X[d])
 
     piece = tokens // HP
 
-    def HID():
+    def HID(i):
         loaded("gate", "up")
 
         def body(r):
-            at = pl.ds(r, 32)
+            at = pl.ds(pl.multiple_of(i * piece + r, 32), 32)
             v = gate_v[at, :].astype(F32)
             hid[0, at, :] = (v / (1.0 + jnp.exp(-v)) * up_v[at, :].astype(F32)).astype(BF16)
 
-        sweep(tokens, 32, body)
+        sweep(piece, 32, body)
 
     def H(i):
         at = pl.ds(i * piece, piece)
         done["h", i] = remote(hid.at[0, at], hid.at[1, at], hs.at[i], hr.at[i], YL)
 
     def M(k, h, q):
-        arrive(("a1", 0, k), ("a1", 1, k))
+        arrive(*(("a1", d, k, part) for d in (0, 1) for part in (0, 1)))
         if q == 1:
             arrive(("a2", 0, k), ("a2", 1, k))
         if h == 1:
@@ -335,11 +352,14 @@
     def E(k, h, q):
         arrive(("oc", k, h, q))
 
-    steps = dict(X1=X1, R=R, X2=X2, X3=X3, Y1=Y1, A2=A2, HID=HID, H=H, M=M, Z0=Z0, Z2=Z2, Z3=Z3, Y2=Y2, O2=O2, O3=O3, E=E)
-    for name, *at in plan():
+    steps = dict(L=L, X1=X1, R=R, X2=X2, X3=X3, Y1=Y1, A2=A2, HID=HID, H=H, M=M, Z0=Z0, Z2=Z2, Z3=Z3, Y2=Y2, O2=O2, O3=O3, E=E)
+    for number, (name, *at) in enumerate(plan()):
+        step_at[0] = number
         steps[name](*at)
-
-    for cp in sends:
+        while settled and settled[0][0] <= number - LATER:
+            settled.pop(0)[1].wait_send()
+
+    for _, cp in settled:
         cp.wait_send()
 
 
@@ -379,8 +399,7 @@
         ),
         in_specs=[hbm] * 6,
         scratch_shapes=[
-            vm((2, rows, block), BF16),
-            vm((2, rows, block), BF16),
+            vm((4, 2, K, rows, LANES), BF16),
             vm((2, K, rows, LANES), BF16),
             vm((2, K, 2, rows, LANES), BF16),
             vm((K, rows, LANES), BF16),
@@ -397,9 +416,9 @@
             vm((2, K, 2, 2, tokens // 8, block // 2), BF16),
             vm((K, 2, 2, tokens // 8, block // 2), BF16),
             vm((3, K, 2, tokens // 8, block // 2), BF16),
-            dma((9,)),
-            *pair((2, K)), *pair((2, K)), *pair((2, K)), *pair((K,)),
-            *pair((2, K)), *pair((2, K)), *pair((HP,)),
+            dma((4, 2, K)), dma((5,)),
+            *pair((2, K)), *pair((2, K)), *pair((2, K, 2)), *pair((K, 2)),
+            *pair((2, K, 2)), *pair((2, K)), *pair((HP,)),
             *pair((K, 2, 2)), *pair((2, K, 2, 2)), *pair((2, K, 2, 2)), *pair((2, K, 2, 2)),
             *pair((3, K, 2)), *pair((2, K, 2, 2)), *pair((2, K, 2, 2)), *pair((K, 2, 2)),
         ],

time: 142 us -> 141 us (level)
  Pallas kernels: 142 us -> 140 us
    pallas_call x1, Pallas kernels: 138 us -> 136 us  [per_device(): pl.pallas_call(kernel, out_shape=(vm(master.shape, F32), vm((K, 2, 2, tok...]
where the time goes in v4:
time: 141 us
  Pallas kernels  140 us (99%)
    pallas_call x1, Pallas kernels, per_device(): pl.pallas_call(kernel, out_shape=(vm(master.shape, F32), vm((K, 2, 2, tok...  136 us
    pallas_call x1, Pallas kernels, per_device(): pl.pallas_call(place, out_shape=(jax.ShapeDtypeStruct(master.shape, F32),...  4.1 us

profile of v4, /device:TPU:1, one launch (start us, length us, event | category | flops | bytes accessed | tf_op | source)
XLA Modules:
  0.0 140.7 jit_solution(10362564181418977967)
XLA Ops:
  0.6 135.8 %handover.1 = (f32[896,512]{1,0:T(8,128)S(1)}, bf16[4,2,2,1024,256]{4,3,2,1,0:T(8,128)(2,1)S(1)}) custom-call(bf16[1,896,4096]{2,1,0:T(8,128)(2,1)} %g.1, f32[896,512]{1,0:T(8,128)} %mst.1, f32[896,512]{1,0:T(8,128)} %mom.1, f32[896,512]{1,0:T(8,128)} %sqr.1, bf16[1024,896]{1,0:T(8,128)(2,1)} %gate.1, bf16[1024,896]{1,0:T(8,128)(2,1)} %up.1), custom_call_target="tpu_custom_call" | custom-call | tf_op jit(solution)/shard_map/handover/pallas_call | solution.py:394
  136.4 4.1 %place.1 = (f32[896,512]{1,0:T(8,128)}, bf16[1024,4096]{1,0:T(8,128)(2,1)}) custom-call(f32[896,512]{1,0:T(8,128)S(1)} %get-tuple-element.4.nm, bf16[4,2,2,1024,256]{4,3,2,1,0:T(8,128)(2,1)S(1)} %get-tuple-element.5.out), custom_call_target="tpu_custom_call" | custom-call | tf_op jit(solution)/shard_map/place/pallas_call | solution.py:430

commit v5 on v4

--- a/solution.py
+++ b/solution.py
@@ -38,36 +38,36 @@
 
 def plan():
     return [
-        ("X1", 1), ("HID", 6), ("H", 6), ("HID", 4), ("HID", 2), ("L", 1), ("H", 4), ("HID", 3), ("R", 1),
-        ("L", 0), ("X1", 2), ("X2", 1, 0), ("H", 3), ("HID", 1), ("L", 2), ("X2", 1, 1), ("HID", 5), ("R", 2),
-        ("H", 2), ("HID", 7), ("X3", 1, 0), ("X2", 2, 0), ("X2", 2, 1), ("X3", 1, 1), ("H", 7), ("Y1", 1, 1),
-        ("X3", 2, 0), ("HID", 0), ("Y1", 1, 0), ("X1", 0), ("X3", 2, 1), ("H", 0), ("M", 1, 0, 0), ("A2", 1, 0),
-        ("A2", 1, 1), ("H", 1), ("Y1", 2, 0), ("Y1", 2, 1), ("Z0", 1, 0, 0), ("R", 0), ("H", 5), ("X2", 0, 0),
-        ("Z2", 1, 0, 0), ("M", 1, 0, 1), ("X2", 0, 1), ("Z3", 1, 0, 0), ("Z0", 1, 0, 1), ("A2", 2, 0),
-        ("M", 2, 0, 0), ("Z2", 1, 0, 1), ("A2", 2, 1), ("X1", 3), ("Z0", 2, 0, 0), ("M", 1, 1, 1),
-        ("Z3", 1, 0, 1), ("Y2", 1, 0, 0), ("M", 2, 1, 0), ("Z2", 2, 0, 0), ("Z0", 1, 1, 1), ("X3", 0, 0),
-        ("Z0", 2, 1, 0), ("M", 1, 1, 0), ("X3", 0, 1), ("Y2", 1, 0, 1), ("Z3", 2, 0, 0), ("Z0", 1, 1, 0),
-        ("Z2", 1, 1, 1), ("O2", 1, 0, 0), ("Z2", 2, 1, 0), ("M", 2, 0, 1), ("Y1", 0, 0), ("O2", 1, 0, 1),
-        ("M", 2, 1, 1), ("Z2", 1, 1, 0), ("Y1", 0, 1), ("Z0", 2, 0, 1), ("O3", 1, 0, 0), ("Z3", 1, 1, 1),
-        ("R", 3), ("Z0", 2, 1, 1), ("X2", 3, 1), ("Z3", 2, 1, 0), ("Y2", 2, 0, 0), ("Z3", 1, 1, 0),
-        ("X2", 3, 0), ("Z2", 2, 0, 1), ("Y2", 1, 1, 1), ("A2", 0, 1), ("Z2", 2, 1, 1), ("M", 0, 0, 0),
-        ("Y2", 2, 1, 0), ("M", 0, 1, 0), ("Z0", 0, 0, 0), ("Z3", 2, 0, 1), ("A2", 0, 0), ("Z0", 0, 1, 0),
-        ("Z3", 2, 1, 1), ("Y2", 1, 1, 0), ("Z2", 0, 0, 0), ("X3", 3, 1), ("Z2", 0, 1, 0), ("Y2", 2, 0, 1),
-        ("Y2", 2, 1, 1), ("O2", 1, 1, 1), ("X3", 3, 0), ("Z3", 0, 0, 0), ("O2", 2, 1, 0), ("O2", 2, 0, 0),
-        ("Z3", 0, 1, 0), ("O2", 1, 1, 0), ("Y1", 3, 1), ("M", 0, 0, 1), ("O2", 2, 1, 1), ("O2", 2, 0, 1),
-        ("Y1", 3, 0), ("Z0", 0, 0, 1), ("M", 0, 1, 1), ("Y2", 0, 0, 0), ("Y2", 0, 1, 0), ("A2", 3, 1),
-        ("Z0", 0, 1, 1), ("Z2", 0, 0, 1), ("O3", 2, 0, 0), ("A2", 3, 0), ("M", 3, 0, 0), ("O2", 0, 0, 0),
-        ("M", 3, 1, 0), ("Z0", 3, 0, 0), ("O2", 0, 1, 0), ("Z2", 0, 1, 1), ("Z0", 3, 1, 0), ("Z3", 0, 0, 1),
-        ("M", 3, 0, 1), ("Z2", 3, 0, 0), ("M", 3, 1, 1), ("Z0", 3, 0, 1), ("O3", 1, 1, 0), ("E", 2, 0, 0),
-        ("O3", 2, 1, 1), ("Z3", 0, 1, 1), ("Z2", 3, 1, 0), ("Z0", 3, 1, 1), ("Z3", 3, 0, 0), ("Z2", 3, 0, 1),
-        ("Y2", 0, 0, 1), ("Z3", 3, 1, 0), ("E", 1, 0, 0), ("Z2", 3, 1, 1), ("Y2", 0, 1, 1), ("Z3", 3, 0, 1),
-        ("E", 2, 1, 1), ("O3", 2, 1, 0), ("Y2", 3, 0, 0), ("Z3", 3, 1, 1), ("O3", 1, 0, 1), ("Y2", 3, 1, 0),
-        ("O2", 0, 1, 1), ("E", 1, 0, 1), ("Y2", 3, 0, 1), ("O3", 0, 1, 0), ("O3", 1, 1, 1), ("Y2", 3, 1, 1),
-        ("O2", 0, 0, 1), ("O2", 3, 0, 0), ("O3", 0, 0, 0), ("E", 2, 1, 0), ("O2", 3, 1, 0), ("O3", 0, 1, 1),
-        ("O2", 3, 0, 1), ("O2", 3, 1, 1), ("O3", 2, 0, 1), ("O3", 0, 0, 1), ("E", 0, 1, 1), ("O3", 3, 0, 0),
-        ("E", 1, 1, 0), ("O3", 3, 1, 0), ("E", 2, 0, 1), ("E", 0, 0, 0), ("E", 0, 1, 0), ("O3", 3, 0, 1),
-        ("O3", 3, 1, 1), ("E", 0, 0, 1), ("E", 3, 1, 0), ("E", 3, 0, 0), ("E", 1, 1, 1), ("E", 3, 0, 1),
-        ("E", 3, 1, 1),
+        ("X1", 1), ("HID", 2), ("H", 2), ("HID", 6), ("HID", 3), ("L", 1), ("HID", 7), ("HID", 1), ("L", 2),
+        ("H", 1), ("R", 1), ("L", 0), ("HID", 4), ("X2", 1, 0), ("X2", 1, 1), ("X1", 3), ("R", 3), ("H", 4),
+        ("X3", 1, 0), ("HID", 0), ("X3", 1, 1), ("HID", 5), ("H", 7), ("Y1", 1, 0), ("H", 0), ("X2", 3, 1),
+        ("X2", 3, 0), ("H", 5), ("Y1", 1, 1), ("A2", 1, 0), ("X1", 0), ("X3", 3, 1), ("X3", 3, 0),
+        ("M", 1, 0, 0), ("A2", 1, 1), ("H", 3), ("H", 6), ("Z0", 1, 0, 0), ("Y1", 3, 1), ("Y1", 3, 0),
+        ("Z2", 1, 0, 0), ("M", 1, 0, 1), ("R", 0), ("Z0", 1, 0, 1), ("X2", 0, 1), ("X2", 0, 0), ("A2", 3, 1),
+        ("Z3", 1, 0, 0), ("M", 3, 0, 0), ("Z2", 1, 0, 1), ("Z0", 3, 0, 0), ("M", 1, 1, 1), ("A2", 3, 0),
+        ("Y2", 1, 0, 0), ("M", 3, 1, 0), ("Z2", 3, 0, 0), ("Z3", 1, 0, 1), ("X1", 2), ("Z0", 1, 1, 1),
+        ("X3", 0, 1), ("Z0", 3, 1, 0), ("M", 1, 1, 0), ("X3", 0, 0), ("Z2", 1, 1, 1), ("Z0", 1, 1, 0),
+        ("Y2", 1, 0, 1), ("Z3", 3, 0, 0), ("M", 3, 0, 1), ("Z2", 3, 1, 0), ("Y1", 0, 1), ("Z2", 1, 1, 0),
+        ("Z3", 1, 1, 1), ("O2", 1, 0, 0), ("Z0", 3, 0, 1), ("Y1", 0, 0), ("M", 3, 1, 1), ("Y2", 3, 0, 0),
+        ("Z3", 3, 1, 0), ("X2", 2, 1), ("R", 2), ("Z3", 1, 1, 0), ("Z0", 3, 1, 1), ("O2", 1, 0, 1),
+        ("Z2", 3, 0, 1), ("O3", 1, 0, 0), ("Y2", 1, 1, 1), ("X2", 2, 0), ("Z2", 3, 1, 1), ("M", 0, 0, 0),
+        ("Y2", 1, 1, 0), ("Y2", 3, 1, 0), ("Z3", 3, 0, 1), ("M", 0, 1, 0), ("Z0", 0, 0, 0), ("O2", 3, 0, 0),
+        ("Z3", 3, 1, 1), ("A2", 0, 0), ("Z0", 0, 1, 0), ("A2", 0, 1), ("X3", 2, 1), ("Z2", 0, 0, 0),
+        ("Y2", 3, 1, 1), ("Y2", 3, 0, 1), ("X3", 2, 0), ("Z2", 0, 1, 0), ("O2", 1, 1, 1), ("O2", 1, 1, 0),
+        ("O2", 3, 1, 0), ("Z3", 0, 0, 0), ("Y1", 2, 1), ("M", 0, 1, 1), ("O2", 3, 1, 1), ("O2", 3, 0, 1),
+        ("Y1", 2, 0), ("Z3", 0, 1, 0), ("Z0", 0, 1, 1), ("M", 0, 0, 1), ("Y2", 0, 0, 0), ("Z0", 0, 0, 1),
+        ("Z2", 0, 1, 1), ("Y2", 0, 1, 0), ("A2", 2, 1), ("A2", 2, 0), ("M", 2, 1, 0), ("O2", 0, 0, 0),
+        ("M", 2, 0, 0), ("Z0", 2, 1, 0), ("Z3", 0, 1, 1), ("Z2", 0, 0, 1), ("O3", 3, 0, 1), ("Z0", 2, 0, 0),
+        ("O2", 0, 1, 0), ("M", 2, 0, 1), ("Z2", 2, 1, 0), ("M", 2, 1, 1), ("Z0", 2, 0, 1), ("Z2", 2, 0, 0),
+        ("O3", 3, 1, 1), ("Z3", 0, 0, 1), ("O3", 0, 1, 0), ("Z0", 2, 1, 1), ("O3", 3, 1, 0), ("Z3", 2, 1, 0),
+        ("Z2", 2, 0, 1), ("O3", 0, 0, 0), ("Y2", 0, 1, 1), ("Z3", 2, 0, 0), ("Z2", 2, 1, 1), ("E", 0, 1, 0),
+        ("E", 3, 1, 1), ("Y2", 0, 0, 1), ("O3", 1, 1, 1), ("Y2", 2, 1, 0), ("Z3", 2, 0, 1), ("Z3", 2, 1, 1),
+        ("Y2", 2, 0, 0), ("E", 3, 1, 0), ("E", 1, 0, 0), ("O2", 0, 0, 1), ("O3", 3, 0, 0), ("Y2", 2, 0, 1),
+        ("Y2", 2, 1, 1), ("O2", 2, 1, 0), ("O3", 1, 1, 0), ("O3", 1, 0, 1), ("E", 3, 0, 1), ("O2", 2, 0, 0),
+        ("O2", 2, 0, 1), ("O2", 0, 1, 1), ("O3", 0, 0, 1), ("E", 1, 1, 0), ("O2", 2, 1, 1), ("O3", 2, 1, 0),
+        ("O3", 2, 0, 0), ("E", 0, 0, 0), ("O3", 2, 0, 1), ("E", 1, 0, 1), ("O3", 0, 1, 1), ("E", 2, 0, 0),
+        ("E", 3, 0, 0), ("O3", 2, 1, 1), ("E", 0, 0, 1), ("E", 1, 1, 1), ("E", 2, 0, 1), ("E", 0, 1, 1),
+        ("E", 2, 1, 0), ("E", 2, 1, 1),
     ]
 
 

time: 141 us -> 140 us (level)
  no operation moved by 1% of the time
where the time goes in v5:
time: 140 us
  Pallas kernels  139 us (99%)
    pallas_call x1, Pallas kernels, per_device(): pl.pallas_call(kernel, out_shape=(vm(master.shape, F32), vm((K, 2, 2, tok...  135 us
    pallas_call x1, Pallas kernels, per_device(): pl.pallas_call(place, out_shape=(jax.ShapeDtypeStruct(master.shape, F32),...  4.1 us

profile of v5, /device:TPU:1, one launch (start us, length us, event | category | flops | bytes accessed | tf_op | source)
XLA Modules:
  0.0 140.0 jit_solution(15470034844762200572)
XLA Ops:
  0.6 135.1 %handover.1 = (f32[896,512]{1,0:T(8,128)S(1)}, bf16[4,2,2,1024,256]{4,3,2,1,0:T(8,128)(2,1)S(1)}) custom-call(bf16[1,896,4096]{2,1,0:T(8,128)(2,1)} %g.1, f32[896,512]{1,0:T(8,128)} %mst.1, f32[896,512]{1,0:T(8,128)} %mom.1, f32[896,512]{1,0:T(8,128)} %sqr.1, bf16[1024,896]{1,0:T(8,128)(2,1)} %gate.1, bf16[1024,896]{1,0:T(8,128)(2,1)} %up.1), custom_call_target="tpu_custom_call" | custom-call | tf_op jit(solution)/shard_map/handover/pallas_call | solution.py:394
  135.7 4.1 %place.1 = (f32[896,512]{1,0:T(8,128)}, bf16[1024,4096]{1,0:T(8,128)(2,1)}) custom-call(f32[896,512]{1,0:T(8,128)S(1)} %get-tuple-element.4.nm, bf16[4,2,2,1024,256]{4,3,2,1,0:T(8,128)(2,1)S(1)} %get-tuple-element.5.out), custom_call_target="tpu_custom_call" | custom-call | tf_op jit(solution)/shard_map/place/pallas_call | solution.py:430

commit v6 on v5

--- a/solution.py
+++ b/solution.py
@@ -38,36 +38,35 @@
 
 def plan():
     return [
-        ("X1", 1), ("HID", 2), ("H", 2), ("HID", 6), ("HID", 3), ("L", 1), ("HID", 7), ("HID", 1), ("L", 2),
-        ("H", 1), ("R", 1), ("L", 0), ("HID", 4), ("X2", 1, 0), ("X2", 1, 1), ("X1", 3), ("R", 3), ("H", 4),
-        ("X3", 1, 0), ("HID", 0), ("X3", 1, 1), ("HID", 5), ("H", 7), ("Y1", 1, 0), ("H", 0), ("X2", 3, 1),
-        ("X2", 3, 0), ("H", 5), ("Y1", 1, 1), ("A2", 1, 0), ("X1", 0), ("X3", 3, 1), ("X3", 3, 0),
-        ("M", 1, 0, 0), ("A2", 1, 1), ("H", 3), ("H", 6), ("Z0", 1, 0, 0), ("Y1", 3, 1), ("Y1", 3, 0),
-        ("Z2", 1, 0, 0), ("M", 1, 0, 1), ("R", 0), ("Z0", 1, 0, 1), ("X2", 0, 1), ("X2", 0, 0), ("A2", 3, 1),
-        ("Z3", 1, 0, 0), ("M", 3, 0, 0), ("Z2", 1, 0, 1), ("Z0", 3, 0, 0), ("M", 1, 1, 1), ("A2", 3, 0),
-        ("Y2", 1, 0, 0), ("M", 3, 1, 0), ("Z2", 3, 0, 0), ("Z3", 1, 0, 1), ("X1", 2), ("Z0", 1, 1, 1),
-        ("X3", 0, 1), ("Z0", 3, 1, 0), ("M", 1, 1, 0), ("X3", 0, 0), ("Z2", 1, 1, 1), ("Z0", 1, 1, 0),
-        ("Y2", 1, 0, 1), ("Z3", 3, 0, 0), ("M", 3, 0, 1), ("Z2", 3, 1, 0), ("Y1", 0, 1), ("Z2", 1, 1, 0),
-        ("Z3", 1, 1, 1), ("O2", 1, 0, 0), ("Z0", 3, 0, 1), ("Y1", 0, 0), ("M", 3, 1, 1), ("Y2", 3, 0, 0),
-        ("Z3", 3, 1, 0), ("X2", 2, 1), ("R", 2), ("Z3", 1, 1, 0), ("Z0", 3, 1, 1), ("O2", 1, 0, 1),
-        ("Z2", 3, 0, 1), ("O3", 1, 0, 0), ("Y2", 1, 1, 1), ("X2", 2, 0), ("Z2", 3, 1, 1), ("M", 0, 0, 0),
-        ("Y2", 1, 1, 0), ("Y2", 3, 1, 0), ("Z3", 3, 0, 1), ("M", 0, 1, 0), ("Z0", 0, 0, 0), ("O2", 3, 0, 0),
-        ("Z3", 3, 1, 1), ("A2", 0, 0), ("Z0", 0, 1, 0), ("A2", 0, 1), ("X3", 2, 1), ("Z2", 0, 0, 0),
-        ("Y2", 3, 1, 1), ("Y2", 3, 0, 1), ("X3", 2, 0), ("Z2", 0, 1, 0), ("O2", 1, 1, 1), ("O2", 1, 1, 0),
-        ("O2", 3, 1, 0), ("Z3", 0, 0, 0), ("Y1", 2, 1), ("M", 0, 1, 1), ("O2", 3, 1, 1), ("O2", 3, 0, 1),
-        ("Y1", 2, 0), ("Z3", 0, 1, 0), ("Z0", 0, 1, 1), ("M", 0, 0, 1), ("Y2", 0, 0, 0), ("Z0", 0, 0, 1),
-        ("Z2", 0, 1, 1), ("Y2", 0, 1, 0), ("A2", 2, 1), ("A2", 2, 0), ("M", 2, 1, 0), ("O2", 0, 0, 0),
-        ("M", 2, 0, 0), ("Z0", 2, 1, 0), ("Z3", 0, 1, 1), ("Z2", 0, 0, 1), ("O3", 3, 0, 1), ("Z0", 2, 0, 0),
-        ("O2", 0, 1, 0), ("M", 2, 0, 1), ("Z2", 2, 1, 0), ("M", 2, 1, 1), ("Z0", 2, 0, 1), ("Z2", 2, 0, 0),
-        ("O3", 3, 1, 1), ("Z3", 0, 0, 1), ("O3", 0, 1, 0), ("Z0", 2, 1, 1), ("O3", 3, 1, 0), ("Z3", 2, 1, 0),
-        ("Z2", 2, 0, 1), ("O3", 0, 0, 0), ("Y2", 0, 1, 1), ("Z3", 2, 0, 0), ("Z2", 2, 1, 1), ("E", 0, 1, 0),
-        ("E", 3, 1, 1), ("Y2", 0, 0, 1), ("O3", 1, 1, 1), ("Y2", 2, 1, 0), ("Z3", 2, 0, 1), ("Z3", 2, 1, 1),
-        ("Y2", 2, 0, 0), ("E", 3, 1, 0), ("E", 1, 0, 0), ("O2", 0, 0, 1), ("O3", 3, 0, 0), ("Y2", 2, 0, 1),
-        ("Y2", 2, 1, 1), ("O2", 2, 1, 0), ("O3", 1, 1, 0), ("O3", 1, 0, 1), ("E", 3, 0, 1), ("O2", 2, 0, 0),
-        ("O2", 2, 0, 1), ("O2", 0, 1, 1), ("O3", 0, 0, 1), ("E", 1, 1, 0), ("O2", 2, 1, 1), ("O3", 2, 1, 0),
-        ("O3", 2, 0, 0), ("E", 0, 0, 0), ("O3", 2, 0, 1), ("E", 1, 0, 1), ("O3", 0, 1, 1), ("E", 2, 0, 0),
-        ("E", 3, 0, 0), ("O3", 2, 1, 1), ("E", 0, 0, 1), ("E", 1, 1, 1), ("E", 2, 0, 1), ("E", 0, 1, 1),
-        ("E", 2, 1, 0), ("E", 2, 1, 1),
+        ("X1", 3), ("HID", 6), ("R", 3), ("L", 0), ("H", 6), ("HID", 4), ("HID", 7), ("L", 1), ("H", 7),
+        ("HID", 0), ("X2", 3, 1), ("X1", 1), ("H", 0), ("HID", 2), ("L", 2), ("H", 2), ("X3", 3, 1), ("HID", 1),
+        ("HID", 5), ("X2", 3, 0), ("R", 1), ("X2", 1, 0), ("X3", 3, 0), ("X2", 1, 1), ("H", 1), ("Y1", 3, 1),
+        ("HID", 3), ("Y1", 3, 0), ("H", 3), ("X1", 0), ("X3", 1, 0), ("X3", 1, 1), ("A2", 3, 1), ("M", 3, 0, 0),
+        ("H", 5), ("A2", 3, 0), ("Z0", 3, 0, 0), ("H", 4), ("Y1", 1, 0), ("Y1", 1, 1), ("Z2", 3, 0, 0),
+        ("R", 0), ("M", 3, 0, 1), ("X2", 0, 0), ("Z0", 3, 0, 1), ("M", 1, 0, 0), ("X2", 0, 1), ("Z3", 3, 0, 0),
+        ("Z2", 3, 0, 1), ("Z0", 1, 0, 0), ("M", 3, 1, 0), ("M", 3, 1, 1), ("Z3", 3, 0, 1), ("Z2", 1, 0, 0),
+        ("Z0", 3, 1, 0), ("A2", 1, 0), ("A2", 1, 1), ("X1", 2), ("X3", 0, 0), ("Y2", 3, 0, 0), ("M", 1, 1, 0),
+        ("Z0", 3, 1, 1), ("X3", 0, 1), ("Z0", 1, 1, 0), ("Y2", 3, 0, 1), ("Z2", 3, 1, 0), ("Z3", 1, 0, 0),
+        ("M", 1, 0, 1), ("Z2", 3, 1, 1), ("Y1", 0, 0), ("Z2", 1, 1, 0), ("Z0", 1, 0, 1), ("Y1", 0, 1),
+        ("M", 1, 1, 1), ("Y2", 1, 0, 0), ("Z3", 3, 1, 1), ("X2", 2, 0), ("O2", 3, 0, 0), ("Z3", 1, 1, 0),
+        ("R", 2), ("Z2", 1, 0, 1), ("Z0", 1, 1, 1), ("X2", 2, 1), ("Z3", 3, 1, 0), ("O2", 1, 0, 0),
+        ("Y2", 3, 1, 1), ("M", 0, 0, 0), ("Z2", 1, 1, 1), ("Y2", 1, 1, 0), ("M", 0, 1, 0), ("Z3", 1, 0, 1),
+        ("Z0", 0, 0, 0), ("A2", 0, 1), ("Z0", 0, 1, 0), ("Z3", 1, 1, 1), ("Y2", 3, 1, 0), ("O2", 1, 1, 0),
+        ("A2", 0, 0), ("O3", 1, 0, 0), ("X3", 2, 0), ("Z2", 0, 0, 0), ("O3", 3, 0, 0), ("Y2", 1, 1, 1),
+        ("X3", 2, 1), ("Y2", 1, 0, 1), ("Z2", 0, 1, 0), ("O2", 3, 1, 1), ("O2", 3, 0, 1), ("O2", 3, 1, 0),
+        ("Z3", 0, 0, 0), ("Y1", 2, 0), ("M", 0, 0, 1), ("O2", 1, 1, 1), ("Y1", 2, 1), ("O2", 1, 0, 1),
+        ("Z3", 0, 1, 0), ("Z0", 0, 0, 1), ("M", 0, 1, 1), ("A2", 2, 0), ("Y2", 0, 0, 0), ("Z0", 0, 1, 1),
+        ("Z2", 0, 0, 1), ("Y2", 0, 1, 0), ("A2", 2, 1), ("M", 2, 0, 0), ("M", 2, 1, 0), ("Z0", 2, 0, 0),
+        ("O3", 3, 1, 0), ("Z3", 0, 0, 1), ("Z2", 0, 1, 1), ("O2", 0, 0, 0), ("Z0", 2, 1, 0), ("M", 2, 1, 1),
+        ("Z2", 2, 0, 0), ("M", 2, 0, 1), ("Z0", 2, 1, 1), ("Z3", 0, 1, 1), ("Z0", 2, 0, 1), ("O3", 1, 1, 1),
+        ("Z2", 2, 1, 0), ("O3", 3, 0, 1), ("O3", 0, 0, 0), ("Z2", 2, 1, 1), ("Z3", 2, 0, 0), ("Y2", 0, 0, 1),
+        ("Z2", 2, 0, 1), ("Z3", 2, 1, 0), ("Y2", 0, 1, 1), ("Z3", 2, 1, 1), ("O2", 0, 1, 0), ("O3", 1, 0, 1),
+        ("O3", 1, 1, 0), ("Y2", 2, 0, 0), ("O3", 3, 1, 1), ("O2", 0, 0, 1), ("Z3", 2, 0, 1), ("E", 3, 0, 1),
+        ("Y2", 2, 1, 0), ("Y2", 2, 1, 1), ("Y2", 2, 0, 1), ("O2", 2, 1, 0), ("O3", 0, 1, 0), ("O3", 0, 0, 1),
+        ("E", 1, 0, 1), ("O2", 0, 1, 1), ("E", 3, 1, 1), ("O2", 2, 0, 0), ("O2", 2, 1, 1), ("E", 0, 0, 1),
+        ("O2", 2, 0, 1), ("O3", 2, 1, 0), ("O3", 0, 1, 1), ("E", 1, 1, 0), ("O3", 2, 0, 0), ("E", 0, 1, 0),
+        ("E", 3, 0, 0), ("E", 2, 1, 0), ("E", 1, 1, 1), ("E", 0, 0, 0), ("O3", 2, 1, 1), ("E", 3, 1, 0),
+        ("E", 1, 0, 0), ("O3", 2, 0, 1), ("E", 0, 1, 1), ("E", 2, 0, 0), ("E", 2, 1, 1), ("E", 2, 0, 1),
     ]
 
 

time: 140 us -> 141 us (level)
  no operation moved by 1% of the time
where the time goes in v6:
time: 141 us
  Pallas kernels  140 us (99%)
    pallas_call x1, Pallas kernels, per_device(): pl.pallas_call(kernel, out_shape=(vm(master.shape, F32), vm((K, 2, 2, tok...  136 us
    pallas_call x1, Pallas kernels, per_device(): pl.pallas_call(place, out_shape=(jax.ShapeDtypeStruct(master.shape, F32),...  4.1 us

profile of v6, /device:TPU:1, one launch (start us, length us, event | category | flops | bytes accessed | tf_op | source)
XLA Modules:
  0.0 141.0 jit_solution(6897214682044816605)
XLA Ops:
  0.6 136.1 %handover.1 = (f32[896,512]{1,0:T(8,128)S(1)}, bf16[4,2,2,1024,256]{4,3,2,1,0:T(8,128)(2,1)S(1)}) custom-call(bf16[1,896,4096]{2,1,0:T(8,128)(2,1)} %g.1, f32[896,512]{1,0:T(8,128)} %mst.1, f32[896,512]{1,0:T(8,128)} %mom.1, f32[896,512]{1,0:T(8,128)} %sqr.1, bf16[1024,896]{1,0:T(8,128)(2,1)} %gate.1, bf16[1024,896]{1,0:T(8,128)(2,1)} %up.1), custom_call_target="tpu_custom_call" | custom-call | tf_op jit(solution)/shard_map/handover/pallas_call | solution.py:393
  136.7 4.1 %place.1 = (f32[896,512]{1,0:T(8,128)}, bf16[1024,4096]{1,0:T(8,128)(2,1)}) custom-call(f32[896,512]{1,0:T(8,128)S(1)} %get-tuple-element.4.nm, bf16[4,2,2,1024,256]{4,3,2,1,0:T(8,128)(2,1)S(1)} %get-tuple-element.5.out), custom_call_target="tpu_custom_call" | custom-call | tf_op jit(solution)/shard_map/place/pallas_call | solution.py:429
